TPU v7x, 32 devices: a whole 2x2x4 slice. The times are simulated.
32 devices in a mesh: rep: 2 (over y), pool: 16 (over z, x, core).
Axes of the slice: x: 2, y: 2, z: 4, core: 2. Of those that a mesh axis runs over, the one named last changes fastest.
Arguments:
- pool_kv: bfloat16 [128, 8, 16, 256], P(('rep', 'pool')), parts along dimension 0, may hold values from -6 to 6
- prefix_table: int32 [4, 32], P('rep'), parts along dimension 0, may hold values from 0 to 63, as said below
- prefix_count: int32 [4], P('rep'), parts along dimension 0, may hold values from 17 to 32, as said below
- prefill_q: bfloat16 [32, 512, 1024], P(('rep', 'pool')), parts along dimension 0, may hold values from -25 to 25
- prefill_new_kv: bfloat16 [32, 512, 256], P(('rep', 'pool')), parts along dimension 0, may hold values from -6 to 6
- decode_q: bfloat16 [512, 8192], P(('rep', 'pool')), parts along dimension 0, may hold values from -25 to 25
- decode_new: bfloat16 [512, 2048], P(('rep', 'pool')), parts along dimension 0, may hold values from -6 to 6
- decode_cache: bfloat16 [32, 128, 2, 64, 256], P(('rep', 'pool')), parts along dimension 0, may hold values from -6 to 6
- decode_group: int32 [512, 1], P('rep'), parts along dimension 0, may hold values from 0 to 3; in each aligned block of 16 rows (0 to 15, 16 to 31, ...) at most 8 rows name the same one
- cached_len: int32 [512], P('rep'), parts along dimension 0, may hold values from 1 to 64, 8192 in all
Outputs:
- prefill_out: bfloat16 [32, 512, 1024], P(('rep', 'pool')), parts along dimension 0
- decode_out: bfloat16 [512, 8192], P(('rep', 'pool')), parts along dimension 0
There are 2 independent parts, one for each index of `rep`. A program takes and returns all parts, laid end to end along the dimension named above; each array names one. Nothing has to cross between parts.
Inputs may be any that keep to these rules, and one draw needn't show every extreme that they name: prefix_table[g, j] = o * 4 + b names block b of owner o. No block appears twice in the table. Among the first prefix_count[g] entries of a row, every owner holds at most 2; entries from prefix_count[g] on are not read. `prefix_count`: at least one request has 32 blocks. `decode_group`: among the rows of one home device, no group is named by more than 8 rows.
All inputs are finite; a program needn't handle non-finite values.
Results may differ from a plain program's by a relative error of at most 0.0055.
Values may be sent and summed in bfloat16 or wider, within the bound.
No kernel may reach another device: no remote copies, remote signals or barrier semaphores. Data moves between devices by JAX's collectives and lax.ppermute only.
A program may use at most 128 MiB of HBM per device.

v0:
```python
import functools

import jax
import jax.numpy as jnp
from jax import lax
from jax.experimental import pallas as pl
from jax.experimental.pallas import tpu as pltpu
from jax.sharding import PartitionSpec as P

PGRP = 8
DGRP = 4
PCAP = 2
LANES = 128
MASKED = -1e30
LOG2E = 1.4426950408889634


def up16(n):
    return -(-n // 16) * 16


def any_spec():
    return pl.BlockSpec(memory_space=pl.ANY)


def smem_spec():
    return pl.BlockSpec(memory_space=pltpu.SMEM)


def vmem_spec():
    return pl.BlockSpec(memory_space=pltpu.VMEM)


def pack_kernel(
    layout, table, count, groups, pool, q, kv, out, rows_scr, group_fill, sems
):
    blk, cap, head_rows, own_rows, q_start, own_start = layout
    blocks_here = pool.shape[0]
    group_count, most_blocks = table.shape
    decode_groups = out.shape[0] // DGRP
    row_count = q.shape[0]
    head_total = q.shape[1] // LANES
    device = lax.axis_index("pool")
    first_block = device * blocks_here
    copies = []
    for g in range(group_count):

        def scan_table(j, carry):
            seen, chosen = carry
            entry = table[g, j]
            mine = (entry >= first_block) & (entry < first_block + blocks_here) & (j < count[g])
            chosen = tuple(
                jnp.where(mine & (seen == k), entry - first_block, chosen[k]) for k in range(PCAP)
            )
            return seen + mine.astype(jnp.int32), chosen

        start = (jnp.int32(0), tuple(jnp.int32(0) for _ in range(PCAP)))
        _, chosen = lax.fori_loop(0, most_blocks, scan_table, start, unroll=8)
        for k in range(PCAP):
            for part in range(2):
                copy = pltpu.make_async_copy(
                    pool.at[chosen[k], :, :, pl.ds(part * LANES, LANES)],
                    out.at[pl.ds(g * PGRP, PGRP), pl.ds((k * 2 + part) * blk, blk), :],
                    sems.at[(g * PCAP + k) * 2 + part],
                )
                copy.start()
                copies.append(copy)
    for a in range(decode_groups):
        group_fill[a] = 0
    for h in range(head_total):
        rows_scr[pl.ds(h, row_count, stride=head_total), :] = q[
            :, h * LANES : (h + 1) * LANES
        ].astype(jnp.float32)
    slot_axis = lax.broadcasted_iota(jnp.int32, (decode_groups * cap, row_count), 0)
    row_axis = lax.broadcasted_iota(jnp.int32, (decode_groups * cap, row_count), 1)
    slot_of_row = jnp.full((decode_groups * cap, row_count), -1, jnp.int32)
    for i in range(row_count):
        a = groups[device * row_count + i]
        c = group_fill[a]
        group_fill[a] = c + 1
        slot_of_row = jnp.where(row_axis == i, a * cap + c, slot_of_row)
        for m in range(DGRP):
            first = i * head_total + m * head_rows
            out[a * DGRP + m, pl.ds(q_start + pl.multiple_of(c * head_rows, 16), head_rows), :] = (
                rows_scr[first : first + head_rows, :].astype(out.dtype)
            )
    pick = (slot_of_row == slot_axis).astype(jnp.bfloat16)
    own = jnp.dot(pick, kv[...], preferred_element_type=jnp.float32)
    pair_count = kv.shape[1] // (2 * LANES * DGRP)
    blank = jnp.zeros((own_rows - pair_count * cap, LANES), jnp.float32)
    for a in range(decode_groups):
        for m in range(DGRP):
            for part in range(2):
                pieces = [
                    own[
                        a * cap : (a + 1) * cap,
                        ((m * pair_count + k) * 2 + part) * LANES : ((m * pair_count + k) * 2 + part + 1) * LANES,
                    ]
                    for k in range(pair_count)
                ]
                if blank.shape[0]:
                    pieces.append(blank)
                out[
                    a * DGRP + m,
                    own_start + part * own_rows : own_start + (part + 1) * own_rows,
                    :,
                ] = jnp.concatenate(pieces, axis=0).astype(out.dtype)
    for copy in copies:
        copy.wait()


def plan_kernel(cap, step, owners, table, count, groups, lengths, slot_len, listed, prefix_held):
    device = lax.axis_index("pool")
    home_count = owners
    row_count = groups.shape[0] // home_count
    group_id = device // DGRP
    prefill_id = device // PGRP
    blocks_here = listed.shape[0]
    most_blocks = table.shape[1]
    chunk = min(cap, step)

    def one_owner(o, carry):
        prefix_held[o] = 0
        return carry

    lax.fori_loop(0, owners, one_owner, 0)
    pool_blocks = prefix_held.shape[0] // owners

    def one_entry(j, carry):
        o = table[prefill_id, j] // pool_blocks
        prefix_held[o] = prefix_held[o] + 1
        return carry

    lax.fori_loop(0, jnp.minimum(count[prefill_id], most_blocks), one_entry, 0)

    def one_home(s, filled):
        for c in range(cap):
            slot_len[s * cap + c] = 0
        here = jnp.int32(0)
        for i in range(row_count):
            row = s * row_count + i
            mine = groups[row] == group_id
            place = s * cap + jnp.minimum(here, cap - 1)
            slot_len[place] = jnp.where(mine, lengths[row], slot_len[place])
            here = here + mine.astype(jnp.int32)
        for b in range(cap // chunk):
            listed[1 + jnp.minimum(filled, blocks_here - 2)] = s * (cap // chunk) + b
            filled = filled + (here > b * chunk).astype(jnp.int32)
        return filled

    listed[0] = lax.fori_loop(0, home_count, one_home, jnp.int32(0))


def decode_kernel(layout, chunk, width, listed, slot_len, recv, cache, out, held, sems):
    blk, cap, head_rows, own_rows, q_start, own_start = layout
    pair_count, positions = cache.shape[1], cache.shape[2]
    per_home = cap // chunk
    key_count = pair_count * positions
    query_heads = head_rows // pair_count
    live = listed[0]
    scale = LANES ** (-0.5) * LOG2E
    rows = chunk * head_rows
    slots = width * chunk

    def fetch(i):
        return pltpu.make_async_copy(
            cache.at[pl.ds(listed[1 + i] * chunk, chunk)],
            held.at[pl.ds(i * chunk, chunk)],
            sems.at[i],
        )

    def begin(i, carry):
        fetch(i).start()
        return carry

    lax.fori_loop(0, live, begin, 0)
    row_pair = lax.broadcasted_iota(jnp.int32, (head_rows, key_count), 0) // query_heads
    key_axis = lax.broadcasted_iota(jnp.int32, (head_rows, key_count), 1)
    pos = jnp.where(key_axis // positions == row_pair, key_axis % positions, positions)
    own_axis = lax.broadcasted_iota(jnp.int32, (rows, own_rows), 1)
    own_row = lax.broadcasted_iota(jnp.int32, (rows, own_rows), 0)
    own_want = ((own_row % head_rows) // query_heads) * cap + own_row // head_rows

    def several(t, carry):
        ids = [jnp.minimum(t * width + w, live - 1) for w in range(width)]
        for w in range(width):

            @pl.when(t * width + w < live)
            def _():
                fetch(t * width + w).wait()

        blocks = [listed[1 + i] for i in ids]
        homes = [b // per_home for b in blocks]
        firsts = [(b % per_home) * chunk for b in blocks]
        places = [pl.multiple_of(f * head_rows, 16) for f in firsts]
        q = jnp.concatenate(
            [recv[h, pl.ds(q_start + p, rows), :] for h, p in zip(homes, places)], axis=0
        )
        own_keys = jnp.stack([recv[h, own_start : own_start + own_rows, :] for h in homes])
        own_values = jnp.stack(
            [recv[h, own_start + own_rows : own_start + 2 * own_rows, :] for h in homes]
        )
        kv = held[pl.ds(t * slots, slots)]
        keys = kv[..., :LANES].reshape(slots, key_count, LANES)
        values = kv[..., LANES:].reshape(slots, key_count, LANES)
        scores = jnp.einsum(
            "jqd,jkd->jqk",
            q.reshape(slots, head_rows, LANES),
            keys,
            preferred_element_type=jnp.float32,
        )
        kept = jnp.stack(
            [pos < slot_len[blocks[w] * chunk + j] for w in range(width) for j in range(chunk)]
        )
        scores = jnp.where(kept, scores, MASKED)
        own_scores = jnp.einsum(
            "jqd,jkd->jqk",
            q.reshape(width, rows, LANES),
            own_keys,
            preferred_element_type=jnp.float32,
        )
        own_hit = jnp.stack([own_axis == own_want + f for f in firsts])
        own_score = jnp.sum(jnp.where(own_hit, own_scores, 0.0), axis=2, keepdims=True)
        own_score = own_score.reshape(slots, head_rows, 1)
        top = jnp.maximum(jnp.max(scores, axis=2, keepdims=True), own_score)
        weights = jnp.exp2((scores - top) * scale)
        own_weight = jnp.exp2((own_score - top) * scale)
        total = jnp.sum(weights, axis=2, keepdims=True) + own_weight
        mixed = jnp.einsum(
            "jqk,jkd->jqd",
            weights.astype(jnp.bfloat16),
            values,
            preferred_element_type=jnp.float32,
        )
        own_part = jnp.where(own_hit, own_weight.reshape(width, rows, 1), 0.0)
        mixed = mixed.reshape(width, rows, LANES) + jnp.einsum(
            "jqk,jkd->jqd",
            own_part.astype(jnp.bfloat16),
            own_values,
            preferred_element_type=jnp.float32,
        )
        mixed = mixed / total.reshape(width, rows, 1)
        for w in reversed(range(width)):
            out[homes[w], pl.ds(places[w], rows), :] = mixed[w].astype(out.dtype)
        return carry

    lax.fori_loop(0, (live + width - 1) // width, several, 0)


def prefill_kernel(layout, tile, prefix_held, recv, q, new_kv, out, keys, values, bias):
    blk = layout[0]
    owners = recv.shape[0]
    prefix = owners * PCAP * blk
    token_count = new_kv.shape[0]
    scale = LANES ** (-0.5) * LOG2E

    @pl.when(pl.program_id(0) == 0)
    def _():
        lane_block = lax.broadcasted_iota(jnp.int32, (8, prefix), 1) // blk
        hide = jnp.zeros((8, prefix), jnp.float32)
        for o in range(owners):
            for k in range(PCAP):
                place = (o * PCAP + k) * blk
                keys[place : place + blk, :] = recv[o, (k * 2) * blk : (k * 2 + 1) * blk, :]
                values[place : place + blk, :] = recv[o, (k * 2 + 1) * blk : (k * 2 + 2) * blk, :]
                gone = jnp.where(prefix_held[o] > k, 0.0, MASKED)
                hide = jnp.where(lane_block == o * PCAP + k, gone, hide)
        bias[...] = hide
        keys[prefix:, :] = new_kv[:, :LANES]
        values[prefix:, :] = new_kv[:, LANES:]

    for t in range(token_count // tile):
        width = prefix + (t + 1) * tile
        block = q[t * tile : (t + 1) * tile, :]
        scores = lax.dot_general(
            block, keys[:width, :], (((1,), (1,)), ((), ())), preferred_element_type=jnp.float32
        )
        causal = lax.broadcasted_iota(jnp.int32, (tile, tile), 0) >= lax.broadcasted_iota(
            jnp.int32, (tile, tile), 1
        )
        pieces = [scores[:, :prefix] + bias[0:1, :]]
        if t:
            pieces.append(scores[:, prefix : width - tile])
        pieces.append(jnp.where(causal, scores[:, width - tile :], MASKED))
        scores = jnp.concatenate(pieces, axis=1)
        top = jnp.max(scores, axis=1, keepdims=True)
        weights = jnp.exp2((scores - top) * scale)
        total = jnp.sum(weights, axis=1, keepdims=True)
        mixed = jnp.dot(
            weights.astype(jnp.bfloat16), values[:width, :], preferred_element_type=jnp.float32
        )
        out[t * tile : (t + 1) * tile, :] = (mixed / total).astype(out.dtype)


def unpack_kernel(cap, head_rows, groups, back, out, rows_scr, group_fill):
    device = lax.axis_index("pool")
    row_count = out.shape[0]
    head_total = out.shape[1] // LANES
    for a in range(back.shape[0] // DGRP):
        group_fill[a] = 0
    for i in range(row_count):
        a = groups[device * row_count + i]
        c = group_fill[a]
        group_fill[a] = c + 1
        for m in range(DGRP):
            first = i * head_total + m * head_rows
            rows_scr[first : first + head_rows, :] = back[
                a * DGRP + m, pl.ds(pl.multiple_of(c * head_rows, 16), head_rows), :
            ].astype(jnp.float32)
    for h in range(head_total):
        out[:, h * LANES : (h + 1) * LANES] = rows_scr[
            pl.ds(h, row_count, stride=head_total), :
        ].astype(out.dtype)


def shards(
    pool_kv,
    prefix_table,
    prefix_count,
    prefill_q,
    prefill_new_kv,
    decode_q,
    decode_new,
    decode_cache,
    decode_group,
    cached_len,
):
    devices = lax.axis_size("pool")
    blk = pool_kv.shape[2]
    row_count, q_width = decode_q.shape
    cap = decode_cache.shape[1] // devices
    decode_groups = devices // DGRP
    pair_count = decode_cache.shape[2]
    head_rows = q_width // LANES // DGRP
    own_rows = up16(pair_count * cap)
    q_start = PCAP * 2 * blk
    own_start = q_start + cap * head_rows
    message_rows = own_start + 2 * own_rows
    layout = (blk, cap, head_rows, own_rows, q_start, own_start)
    groups = decode_group.reshape(-1)
    prefill_groups = prefix_table.shape[0]
    big = pltpu.CompilerParams(vmem_limit_bytes=60 * 2**20)
    part = pltpu.CompilerParams(vmem_limit_bytes=52 * 2**20)
    small = pltpu.CompilerParams(vmem_limit_bytes=8 * 2**20)

    sending = pl.pallas_call(
        functools.partial(pack_kernel, layout),
        out_shape=jax.ShapeDtypeStruct((devices, message_rows, LANES), jnp.bfloat16),
        in_specs=[smem_spec(), smem_spec(), smem_spec(), any_spec(), vmem_spec(), vmem_spec()],
        out_specs=vmem_spec(),
        scratch_shapes=[
            pltpu.VMEM((row_count * q_width // LANES, LANES), jnp.float32),
            pltpu.SMEM((decode_groups,), jnp.int32),
            pltpu.SemaphoreType.DMA((prefill_groups * PCAP * 2,)),
        ],
        compiler_params=big,
        name="pack",
    )(prefix_table, prefix_count, groups, pool_kv, decode_q, decode_new)

    received = lax.all_to_all(sending, "pool", split_axis=0, concat_axis=0, tiled=True)

    chunk = min(cap, 4)
    width = 8
    block_count = devices * cap // chunk
    slot_len, listed, prefix_held = pl.pallas_call(
        functools.partial(plan_kernel, cap, chunk, devices),
        out_shape=(
            jax.ShapeDtypeStruct((devices * cap,), jnp.int32),
            jax.ShapeDtypeStruct((block_count + 2,), jnp.int32),
            jax.ShapeDtypeStruct((devices * pool_kv.shape[0],), jnp.int32),
        ),
        in_specs=[smem_spec()] * 4,
        out_specs=(smem_spec(),) * 3,
        compiler_params=big,
        cost_estimate=pl.CostEstimate(flops=1000000, bytes_accessed=4000000, transcendentals=0),
        name="plan",
    )(prefix_table, prefix_count, groups, cached_len)

    answers = pl.pallas_call(
        functools.partial(decode_kernel, layout, chunk, width),
        out_shape=jax.ShapeDtypeStruct((devices, cap * head_rows, LANES), jnp.bfloat16),
        in_specs=[smem_spec(), smem_spec(), vmem_spec(), any_spec()],
        out_specs=vmem_spec(),
        scratch_shapes=[
            pltpu.VMEM((block_count * chunk,) + decode_cache.shape[2:], jnp.bfloat16),
            pltpu.SemaphoreType.DMA((block_count,)),
        ],
        compiler_params=part,
        cost_estimate=pl.CostEstimate(
            flops=500000000, bytes_accessed=8000000, transcendentals=1000000
        ),
        name="decode",
    )(listed, slot_len, received, decode_cache[0])

    back = lax.all_to_all(answers, "pool", split_axis=0, concat_axis=0, tiled=True)

    token_count, fill_width = prefill_q.shape[1:]
    prefix = devices * PCAP * blk
    head_count = fill_width // LANES
    prefix_held, received, _ = lax.optimization_barrier((prefix_held, received, answers))
    prefill_out = pl.pallas_call(
        functools.partial(prefill_kernel, layout, min(256, token_count)),
        grid=(head_count,),
        out_shape=jax.ShapeDtypeStruct((token_count, fill_width), jnp.bfloat16),
        in_specs=[
            smem_spec(),
            pl.BlockSpec((devices, PCAP * 2 * blk, LANES), lambda u: (0, 0, 0)),
            pl.BlockSpec((token_count, LANES), lambda u: (0, u)),
            pl.BlockSpec(prefill_new_kv.shape[1:], lambda u: (0, 0)),
        ],
        out_specs=pl.BlockSpec((token_count, LANES), lambda u: (0, u)),
        scratch_shapes=[
            pltpu.VMEM((prefix + token_count, LANES), jnp.bfloat16),
            pltpu.VMEM((prefix + token_count, LANES), jnp.bfloat16),
            pltpu.VMEM((8, prefix), jnp.float32),
        ],
        compiler_params=pltpu.CompilerParams(vmem_limit_bytes=16 * 2**20),
        cost_estimate=pl.CostEstimate(
            flops=2 * 2 * token_count * fill_width * (prefix + token_count // 2),
            bytes_accessed=3000000,
            transcendentals=token_count * head_count * (prefix + token_count // 2),
        ),
        name="prefill",
    )(prefix_held, received, prefill_q[0], prefill_new_kv[0])

    decode_out = pl.pallas_call(
        functools.partial(unpack_kernel, cap, head_rows),
        out_shape=jax.ShapeDtypeStruct((row_count, q_width), jnp.bfloat16),
        in_specs=[smem_spec(), vmem_spec()],
        out_specs=vmem_spec(),
        scratch_shapes=[
            pltpu.VMEM((row_count * q_width // LANES, LANES), jnp.float32),
            pltpu.SMEM((decode_groups,), jnp.int32),
        ],
        compiler_params=small,
        name="unpack",
    )(groups, back)
    return (prefill_out[None], decode_out)


def solution(mesh):
    in_specs = (
        P(("rep", "pool"), None, None, None),
        P("rep", None),
        P("rep"),
        P(("rep", "pool"), None, None),
        P(("rep", "pool"), None, None),
        P(("rep", "pool"), None),
        P(("rep", "pool"), None),
        P(("rep", "pool"), None, None, None, None),
        P("rep", None),
        P("rep"),
    )
    out_specs = (P(("rep", "pool"), None, None), P(("rep", "pool"), None))
    return jax.shard_map(shards, mesh=mesh, in_specs=in_specs, out_specs=out_specs, check_vma=False)
```

profile of v0, /device:TPU:0, one launch (start us, length us, event | category | flops | bytes accessed | tf_op | source)
XLA Modules:
  0.0 63.7 jit_solution(240694984466578130)
XLA Ops:
  0.6 0.0 copy-start.4
  0.6 0.0 copy-start.3
  0.7 3.3 %pack.1 = bf16[16,224,128]{2,1,0:T(8,128)(2,1)} custom-call(s32[2,32]{1,0:T(2,128)} %table.3, s32[2]{0:T(128)} %count.3, s32[256]{0:T(256)} %bitcast.5, bf16[4,8,16,256]{3,2,1,0:T(8,128)(2,1)} %pool.1, bf16[16,8192]{1,0:T(8,128)(2,1)} %q.1, bf16[16,2048]{1,0:T(8,128)(2,1)} %kv.1), custom_call_target="tpu_custom_call" | custom-call | tf_op jit(solution)/shard_map/pack/pallas_call | solution.py:346
  4.0 7.4 %all-to-all-start = ((bf16[16,224,128]{2,1,0:T(8,128)(2,1)}), bf16[16,224,128]{2,1,0:T(8,128)(2,1)S(1)}, u32[]{:S(2)}, u32[]{:S(2)}) async-start(bf16[16,224,128]{2,1,0:T(8,128)(2,1)} %pack.1), calls=%async_computation | async-start | bytes 1835008 | tf_op jit(solution)/shard_map/all_to_all | solution.py:360
  11.3 2.9 %plan.1 = (s32[128]{0:T(128)}, s32[34]{0:T(128)}, s32[64]{0:T(128)}) custom-call(s32[2,32]{1,0:T(2,128)} %table.3, s32[2]{0:T(128)} %count.3, s32[256]{0:T(256)} %bitcast.6, s32[256]{0:T(256)} %lengths.1), custom_call_target="tpu_custom_call" | custom-call | flops 1000000 | bytes 4000000 | tf_op jit(solution)/shard_map/plan/pallas_call | solution.py:365
  14.2 0.0 copy-start.5
  14.2 17.9 %all-to-all-done.recv = bf16[16,224,128]{2,1,0:T(8,128)(2,1)S(1)} async-done(((bf16[16,224,128]{2,1,0:T(8,128)(2,1)}), bf16[16,224,128]{2,1,0:T(8,128)(2,1)S(1)}, u32[]{:S(2)}, u32[]{:S(2)}) %all-to-all-start) | async-done | bytes 917536 | tf_op jit(solution)/shard_map/all_to_all | solution.py:360
  32.2 0.0 copy-start.1
  32.2 0.7 %copy-done.1 = s32[128]{0:T(128)S(1)} copy-done((s32[128]{0:T(128)S(1)}, s32[128]{0:T(128)}, u32[]{:S(2)}) %copy-start.1) | copy-done | bytes 536
  32.8 0.0 copy-start.2
  32.8 0.6 copy-done.2
  33.4 0.0 copy-start
  33.4 5.6 %decode.1 = bf16[16,128,128]{2,1,0:T(8,128)(2,1)} custom-call(s32[34]{0:T(128)S(1)} %copy-done.2, s32[128]{0:T(128)S(1)} %copy-done.1, bf16[16,224,128]{2,1,0:T(8,128)(2,1)S(1)} %all-to-all-done.recv, bf16[128,2,64,256]{3,2,1,0:T(8,128)(2,1)} %bitcast.10), custom_call_target="tpu_custom_call" | custom-call | flops 500000000 | bytes 8000000 | tf_op jit(solution)/shard_map/decode/pallas_call | solution.py:379
  39.0 8.6 %all-to-all-start.1 = ((bf16[16,128,128]{2,1,0:T(8,128)(2,1)}), bf16[16,128,128]{2,1,0:T(8,128)(2,1)S(1)}, u32[]{:S(2)}, u32[]{:S(2)}) async-start(bf16[16,128,128]{2,1,0:T(8,128)(2,1)} %decode.1), calls=%async_computation.1 | async-start | bytes 1048576 | tf_op jit(solution)/shard_map/all_to_all | solution.py:395
  47.6 0.0 copy-done.4
  47.7 0.0 copy-done.3
  47.7 0.0 copy-done.5
  47.7 10.8 %prefill.1 = bf16[512,1024]{1,0:T(8,128)(2,1)} custom-call(s32[64]{0:T(128)S(1)} %copy-done.5, bf16[16,224,128]{2,1,0:T(8,128)(2,1)S(1)} %all-to-all-done.recv, bf16[512,1024]{1,0:T(8,128)(2,1)S(1)} %bitcast.8, bf16[512,256]{1,0:T(8,128)(2,1)S(1)} %bitcast.9), custom_call_target="tpu_custom_call" | custom-call | flops 1610612736 | bytes 3000000 | tf_op jit(solution)/shard_map/prefill/pallas_call | solution.py:401
  58.5 3.7 %all-to-all-done.1.back = bf16[16,128,128]{2,1,0:T(8,128)(2,1)S(1)} async-done(((bf16[16,128,128]{2,1,0:T(8,128)(2,1)}), bf16[16,128,128]{2,1,0:T(8,128)(2,1)S(1)}, u32[]{:S(2)}, u32[]{:S(2)}) %all-to-all-start.1) | async-done | bytes 524320 | tf_op jit(solution)/shard_map/all_to_all | solution.py:395
  62.1 0.0 copy-done
  62.1 1.6 %unpack.1 = bf16[16,8192]{1,0:T(8,128)(2,1)} custom-call(s32[256]{0:T(256)S(1)} %bitcast.7, bf16[16,128,128]{2,1,0:T(8,128)(2,1)S(1)} %all-to-all-done.1.back), custom_call_target="tpu_custom_call" | custom-call | tf_op jit(solution)/shard_map/unpack/pallas_call | solution.py:426
Async XLA Ops:
  0.6 47.0 %copy-start.4 = (bf16[1,512,256]{2,1,0:T(8,128)(2,1)S(1)}, bf16[1,512,256]{2,1,0:T(8,128)(2,1)}, u32[]{:S(2)}) copy-start(bf16[1,512,256]{2,1,0:T(8,128)(2,1)} %param.14) | copy-start | bytes 786436
  0.6 47.0 %copy-start.3 = (bf16[1,512,1024]{2,1,0:T(8,128)(2,1)S(1)}, bf16[1,512,1024]{2,1,0:T(8,128)(2,1)}, u32[]{:S(2)}) copy-start(bf16[1,512,1024]{2,1,0:T(8,128)(2,1)} %param.13) | copy-start | bytes 3145732
  4.0 28.2 %all-to-all-start = ((bf16[16,224,128]{2,1,0:T(8,128)(2,1)}), bf16[16,224,128]{2,1,0:T(8,128)(2,1)S(1)}, u32[]{:S(2)}, u32[]{:S(2)}) async-start(bf16[16,224,128]{2,1,0:T(8,128)(2,1)} %pack.1), calls=%async_computation | async-start | bytes 1835008 | tf_op jit(solution)/shard_map/all_to_all | solution.py:360
  14.2 33.4 %copy-start.5 = (s32[64]{0:T(128)S(1)}, s32[64]{0:T(128)}, u32[]{:S(2)}) copy-start(s32[64]{0:T(128)} %get-tuple-element.10.prefix_held) | copy-start | bytes 772
  32.2 0.7 %copy-start.1 = (s32[128]{0:T(128)S(1)}, s32[128]{0:T(128)}, u32[]{:S(2)}) copy-start(s32[128]{0:T(128)} %get-tuple-element.9.slot_len) | copy-start | bytes 1540
  32.8 0.6 copy-start.2
  33.4 28.7 %copy-start = (s32[256,1]{0,1:T(1,128)S(1)}, s32[256,1]{0,1:T(1,128)}, u32[]{:S(2)}) copy-start(s32[256,1]{0,1:T(1,128)} %param.18) | copy-start | bytes 3076
  39.0 23.1 %all-to-all-start.1 = ((bf16[16,128,128]{2,1,0:T(8,128)(2,1)}), bf16[16,128,128]{2,1,0:T(8,128)(2,1)S(1)}, u32[]{:S(2)}, u32[]{:S(2)}) async-start(bf16[16,128,128]{2,1,0:T(8,128)(2,1)} %decode.1), calls=%async_computation.1 | async-start | bytes 1048576 | tf_op jit(solution)/shard_map/all_to_all | solution.py:395
where the time goes:
time: 63.7 us
  Pallas kernels  24.2 us (38%)
  waiting for transfers between devices  21.6 us (34%)
  starting transfers between devices  16 us (25%)
  local copies, waits for them, and re-layouts  1.29 us (2%)
  between operations  0.72 us (1%)
    all_to_all x1, waiting for transfers between devices, shards(): lax.all_to_all(sending, 'pool', split_axis=0, concat_axis=0, tiled=True)  17.9 us
    pallas_call x1, Pallas kernels, shards(): pl.pallas_call(functools.partial(prefill_kernel, layout, min(256, token_c...  10.8 us
    all_to_all x1, starting transfers between devices, shards(): lax.all_to_all(answers, 'pool', split_axis=0, concat_axis=0, tiled=True)  8.63 us
    all_to_all x1, starting transfers between devices, shards(): lax.all_to_all(sending, 'pool', split_axis=0, concat_axis=0, tiled=True)  7.37 us
    pallas_call x1, Pallas kernels, shards(): pl.pallas_call(functools.partial(decode_kernel, layout, chunk, width), ou...  5.56 us
    all_to_all x1, waiting for transfers between devices, shards(): lax.all_to_all(answers, 'pool', split_axis=0, concat_axis=0, tiled=True)  3.65 us
    pallas_call x1, Pallas kernels, shards(): pl.pallas_call(functools.partial(pack_kernel, layout), out_shape=jax.Shap...  3.3 us
    pallas_call x1, Pallas kernels, shards(): pl.pallas_call(functools.partial(plan_kernel, cap, chunk, devices), out_s...  2.88 us
  transfers between devices with their start and end apart: 2, of which 2 were waited for; matrix products, arithmetic and copies ran while one was open for 0% of the time, Pallas kernels for 21%

commit v1 on v0

--- a/solution.py
+++ b/solution.py
@@ -31,40 +31,13 @@
     return pl.BlockSpec(memory_space=pltpu.VMEM)
 
 
-def pack_kernel(
-    layout, table, count, groups, pool, q, kv, out, rows_scr, group_fill, sems
-):
-    blk, cap, head_rows, own_rows, q_start, own_start = layout
-    blocks_here = pool.shape[0]
-    group_count, most_blocks = table.shape
-    decode_groups = out.shape[0] // DGRP
+def pack_kernel(layout, groups, q, kv, out, rows_scr, stage, group_fill, sems):
+    cap, head_rows, own_rows, own_start = layout
+    decode_groups = out.shape[0]
     row_count = q.shape[0]
     head_total = q.shape[1] // LANES
+    pair_count = kv.shape[1] // (2 * LANES * DGRP)
     device = lax.axis_index("pool")
-    first_block = device * blocks_here
-    copies = []
-    for g in range(group_count):
-
-        def scan_table(j, carry):
-            seen, chosen = carry
-            entry = table[g, j]
-            mine = (entry >= first_block) & (entry < first_block + blocks_here) & (j < count[g])
-            chosen = tuple(
-                jnp.where(mine & (seen == k), entry - first_block, chosen[k]) for k in range(PCAP)
-            )
-            return seen + mine.astype(jnp.int32), chosen
-
-        start = (jnp.int32(0), tuple(jnp.int32(0) for _ in range(PCAP)))
-        _, chosen = lax.fori_loop(0, most_blocks, scan_table, start, unroll=8)
-        for k in range(PCAP):
-            for part in range(2):
-                copy = pltpu.make_async_copy(
-                    pool.at[chosen[k], :, :, pl.ds(part * LANES, LANES)],
-                    out.at[pl.ds(g * PGRP, PGRP), pl.ds((k * 2 + part) * blk, blk), :],
-                    sems.at[(g * PCAP + k) * 2 + part],
-                )
-                copy.start()
-                copies.append(copy)
     for a in range(decode_groups):
         group_fill[a] = 0
     for h in range(head_total):
@@ -74,37 +47,92 @@
     slot_axis = lax.broadcasted_iota(jnp.int32, (decode_groups * cap, row_count), 0)
     row_axis = lax.broadcasted_iota(jnp.int32, (decode_groups * cap, row_count), 1)
     slot_of_row = jnp.full((decode_groups * cap, row_count), -1, jnp.int32)
+    homes = []
     for i in range(row_count):
         a = groups[device * row_count + i]
         c = group_fill[a]
         group_fill[a] = c + 1
         slot_of_row = jnp.where(row_axis == i, a * cap + c, slot_of_row)
-        for m in range(DGRP):
-            first = i * head_total + m * head_rows
-            out[a * DGRP + m, pl.ds(q_start + pl.multiple_of(c * head_rows, 16), head_rows), :] = (
-                rows_scr[first : first + head_rows, :].astype(out.dtype)
-            )
+        homes.append((a, c))
     pick = (slot_of_row == slot_axis).astype(jnp.bfloat16)
     own = jnp.dot(pick, kv[...], preferred_element_type=jnp.float32)
-    pair_count = kv.shape[1] // (2 * LANES * DGRP)
     blank = jnp.zeros((own_rows - pair_count * cap, LANES), jnp.float32)
-    for a in range(decode_groups):
-        for m in range(DGRP):
+    copies = []
+    for m in range(DGRP):
+        for i, (a, c) in enumerate(homes):
+            first = i * head_total + m * head_rows
+            stage[m, a, pl.ds(pl.multiple_of(c * head_rows, 16), head_rows), :] = rows_scr[
+                first : first + head_rows, :
+            ].astype(out.dtype)
+        for a in range(decode_groups):
             for part in range(2):
-                pieces = [
-                    own[
-                        a * cap : (a + 1) * cap,
-                        ((m * pair_count + k) * 2 + part) * LANES : ((m * pair_count + k) * 2 + part + 1) * LANES,
-                    ]
-                    for k in range(pair_count)
-                ]
+                pieces = []
+                for k in range(pair_count):
+                    lane = ((m * pair_count + k) * 2 + part) * LANES
+                    pieces.append(own[a * cap : (a + 1) * cap, lane : lane + LANES])
                 if blank.shape[0]:
                     pieces.append(blank)
-                out[
-                    a * DGRP + m,
-                    own_start + part * own_rows : own_start + (part + 1) * own_rows,
-                    :,
-                ] = jnp.concatenate(pieces, axis=0).astype(out.dtype)
+                place = own_start + part * own_rows
+                stage[m, a, place : place + own_rows, :] = jnp.concatenate(
+                    pieces, axis=0
+                ).astype(out.dtype)
+        copy = pltpu.make_async_copy(stage.at[m], out.at[:, m], sems.at[m])
+        copy.start()
+        copies.append(copy)
+    for copy in copies:
+        copy.wait()
+
+
+def blocks_kernel(table, count, pool, *rest):
+    outs, sems = rest[:PGRP], rest[PGRP]
+    blocks_here = pool.shape[0]
+    group_count, most_blocks = table.shape
+    device = lax.axis_index("pool")
+    first_block = device * blocks_here
+    flying = []
+    for g in range(group_count):
+
+        def scan_table(j, carry):
+            seen, chosen = carry
+            entry = table[g, j]
+            mine = (entry >= first_block) & (entry < first_block + blocks_here) & (j < count[g])
+            chosen = tuple(
+                jnp.where(mine & (seen == k), entry - first_block, chosen[k]) for k in range(PCAP)
+            )
+            return seen + mine.astype(jnp.int32), chosen
+
+        start = (jnp.int32(0), tuple(jnp.int32(0) for _ in range(PCAP)))
+        _, chosen = lax.fori_loop(0, most_blocks, scan_table, start, unroll=8)
+        if g >= 2:
+            for copy in flying.pop(0):
+                copy.wait()
+        copies = []
+        for t in range(PGRP):
+            for k in range(PCAP):
+                copy = pltpu.make_async_copy(
+                    pool.at[chosen[k], (device % PGRP) ^ t],
+                    outs[t].at[g, k],
+                    sems.at[((g % 2) * PGRP + t) * PCAP + k],
+                )
+                copy.start()
+                copies.append(copy)
+        flying.append(copies)
+    for copies in flying:
+        for copy in copies:
+            copy.wait()
+
+
+def regroup_kernel(group_count, *rest):
+    held, outs, sems = rest[:PGRP], rest[PGRP : PGRP + group_count], rest[-1]
+    mine = lax.axis_index("pool") // PGRP
+    copies = []
+    for x in range(group_count):
+        for t in range(PGRP):
+            copy = pltpu.make_async_copy(
+                held[t].at[(mine + x) % group_count], outs[x].at[t], sems.at[x * PGRP + t]
+            )
+            copy.start()
+            copies.append(copy)
     for copy in copies:
         copy.wait()
 
@@ -152,7 +180,7 @@
 
 
 def decode_kernel(layout, chunk, width, listed, slot_len, recv, cache, out, held, sems):
-    blk, cap, head_rows, own_rows, q_start, own_start = layout
+    cap, head_rows, own_rows, own_start = layout
     pair_count, positions = cache.shape[1], cache.shape[2]
     per_home = cap // chunk
     key_count = pair_count * positions
@@ -194,7 +222,7 @@
         firsts = [(b % per_home) * chunk for b in blocks]
         places = [pl.multiple_of(f * head_rows, 16) for f in firsts]
         q = jnp.concatenate(
-            [recv[h, pl.ds(q_start + p, rows), :] for h, p in zip(homes, places)], axis=0
+            [recv[h, pl.ds(p, rows), :] for h, p in zip(homes, places)], axis=0
         )
         own_keys = jnp.stack([recv[h, own_start : own_start + own_rows, :] for h in homes])
         own_values = jnp.stack(
@@ -247,24 +275,30 @@
     lax.fori_loop(0, (live + width - 1) // width, several, 0)
 
 
-def prefill_kernel(layout, tile, prefix_held, recv, q, new_kv, out, keys, values, bias):
-    blk = layout[0]
-    owners = recv.shape[0]
-    prefix = owners * PCAP * blk
+def prefill_kernel(group_count, tile, prefix_held, *rest):
+    sources = rest[:group_count]
+    q, new_kv, out, keys, values, bias = rest[group_count:]
+    blk = sources[0].shape[2]
+    prefix = group_count * PGRP * PCAP * blk
     token_count = new_kv.shape[0]
     scale = LANES ** (-0.5) * LOG2E
+    device = lax.axis_index("pool")
 
     @pl.when(pl.program_id(0) == 0)
     def _():
         lane_block = lax.broadcasted_iota(jnp.int32, (8, prefix), 1) // blk
         hide = jnp.zeros((8, prefix), jnp.float32)
-        for o in range(owners):
-            for k in range(PCAP):
-                place = (o * PCAP + k) * blk
-                keys[place : place + blk, :] = recv[o, (k * 2) * blk : (k * 2 + 1) * blk, :]
-                values[place : place + blk, :] = recv[o, (k * 2 + 1) * blk : (k * 2 + 2) * blk, :]
-                gone = jnp.where(prefix_held[o] > k, 0.0, MASKED)
-                hide = jnp.where(lane_block == o * PCAP + k, gone, hide)
+        for x in range(group_count):
+            sender = (device // PGRP - x + group_count) % group_count
+            for t in range(PGRP):
+                owner = sender * PGRP + ((device % PGRP) ^ t)
+                for k in range(PCAP):
+                    ordinal = (x * PGRP + t) * PCAP + k
+                    block = sources[x][t, k]
+                    keys[ordinal * blk : (ordinal + 1) * blk, :] = block[:, :LANES]
+                    values[ordinal * blk : (ordinal + 1) * blk, :] = block[:, LANES:]
+                    gone = jnp.where(prefix_held[owner] > k, 0.0, MASKED)
+                    hide = jnp.where(lane_block == ordinal, gone, hide)
         bias[...] = hide
         keys[prefix:, :] = new_kv[:, :LANES]
         values[prefix:, :] = new_kv[:, LANES:]
@@ -333,10 +367,9 @@
     pair_count = decode_cache.shape[2]
     head_rows = q_width // LANES // DGRP
     own_rows = up16(pair_count * cap)
-    q_start = PCAP * 2 * blk
-    own_start = q_start + cap * head_rows
+    own_start = cap * head_rows
     message_rows = own_start + 2 * own_rows
-    layout = (blk, cap, head_rows, own_rows, q_start, own_start)
+    layout = (cap, head_rows, own_rows, own_start)
     groups = decode_group.reshape(-1)
     prefill_groups = prefix_table.shape[0]
     big = pltpu.CompilerParams(vmem_limit_bytes=60 * 2**20)
@@ -345,19 +378,57 @@
 
     sending = pl.pallas_call(
         functools.partial(pack_kernel, layout),
-        out_shape=jax.ShapeDtypeStruct((devices, message_rows, LANES), jnp.bfloat16),
-        in_specs=[smem_spec(), smem_spec(), smem_spec(), any_spec(), vmem_spec(), vmem_spec()],
-        out_specs=vmem_spec(),
+        out_shape=jax.ShapeDtypeStruct((decode_groups, DGRP, message_rows, LANES), jnp.bfloat16),
+        in_specs=[smem_spec(), vmem_spec(), vmem_spec()],
+        out_specs=any_spec(),
         scratch_shapes=[
             pltpu.VMEM((row_count * q_width // LANES, LANES), jnp.float32),
+            pltpu.VMEM((DGRP, decode_groups, message_rows, LANES), jnp.bfloat16),
             pltpu.SMEM((decode_groups,), jnp.int32),
-            pltpu.SemaphoreType.DMA((prefill_groups * PCAP * 2,)),
+            pltpu.SemaphoreType.DMA((DGRP,)),
         ],
         compiler_params=big,
         name="pack",
-    )(prefix_table, prefix_count, groups, pool_kv, decode_q, decode_new)
+    )(groups, decode_q, decode_new)
+    sending = sending.reshape(devices, message_rows, LANES)
 
     received = lax.all_to_all(sending, "pool", split_axis=0, concat_axis=0, tiled=True)
+
+    share = jax.ShapeDtypeStruct((prefill_groups, PCAP, blk, 2 * LANES), jnp.bfloat16)
+    shares = pl.pallas_call(
+        blocks_kernel,
+        out_shape=(share,) * PGRP,
+        in_specs=[smem_spec(), smem_spec(), any_spec()],
+        out_specs=(any_spec(),) * PGRP,
+        scratch_shapes=[pltpu.SemaphoreType.DMA((2 * PGRP * PCAP,))],
+        compiler_params=small,
+        cost_estimate=pl.CostEstimate(flops=100000, bytes_accessed=1000000, transcendentals=0),
+        name="blocks",
+    )(prefix_table, prefix_count, pool_kv)
+    shares = [shares[0]] + [
+        lax.ppermute(shares[t], "pool", [(i, i ^ t) for i in range(devices)])
+        for t in range(1, PGRP)
+    ]
+    bundle = jax.ShapeDtypeStruct((PGRP, PCAP, blk, 2 * LANES), jnp.bfloat16)
+    bundles = pl.pallas_call(
+        functools.partial(regroup_kernel, prefill_groups),
+        out_shape=(bundle,) * prefill_groups,
+        in_specs=[any_spec()] * PGRP,
+        out_specs=(any_spec(),) * prefill_groups,
+        scratch_shapes=[pltpu.SemaphoreType.DMA((prefill_groups * PGRP,))],
+        compiler_params=small,
+        cost_estimate=pl.CostEstimate(flops=100000, bytes_accessed=1000000, transcendentals=0),
+        name="regroup",
+    )(*shares)
+    received, *bundles = lax.optimization_barrier((received, *bundles))
+    bundles = [bundles[0]] + [
+        lax.ppermute(
+            bundles[x],
+            "pool",
+            [(i, (i + x * PGRP) % devices) for i in range(devices)],
+        )
+        for x in range(1, prefill_groups)
+    ]
 
     chunk = min(cap, 4)
     width = 8
@@ -371,7 +442,7 @@
         ),
         in_specs=[smem_spec()] * 4,
         out_specs=(smem_spec(),) * 3,
-        compiler_params=big,
+        compiler_params=small,
         cost_estimate=pl.CostEstimate(flops=1000000, bytes_accessed=4000000, transcendentals=0),
         name="plan",
     )(prefix_table, prefix_count, groups, cached_len)
@@ -392,19 +463,20 @@
         name="decode",
     )(listed, slot_len, received, decode_cache[0])
 
+    answers, *bundles = lax.optimization_barrier((answers, *bundles))
     back = lax.all_to_all(answers, "pool", split_axis=0, concat_axis=0, tiled=True)
 
     token_count, fill_width = prefill_q.shape[1:]
     prefix = devices * PCAP * blk
     head_count = fill_width // LANES
-    prefix_held, received, _ = lax.optimization_barrier((prefix_held, received, answers))
+    prefix_held, _ = lax.optimization_barrier((prefix_held, answers))
     prefill_out = pl.pallas_call(
-        functools.partial(prefill_kernel, layout, min(256, token_count)),
+        functools.partial(prefill_kernel, prefill_groups, min(256, token_count)),
         grid=(head_count,),
         out_shape=jax.ShapeDtypeStruct((token_count, fill_width), jnp.bfloat16),
-        in_specs=[
-            smem_spec(),
-            pl.BlockSpec((devices, PCAP * 2 * blk, LANES), lambda u: (0, 0, 0)),
+        in_specs=[smem_spec()]
+        + [pl.BlockSpec(bundle.shape, lambda u: (0, 0, 0, 0))] * prefill_groups
+        + [
             pl.BlockSpec((token_count, LANES), lambda u: (0, u)),
             pl.BlockSpec(prefill_new_kv.shape[1:], lambda u: (0, 0)),
         ],
@@ -421,7 +493,7 @@
             transcendentals=token_count * head_count * (prefix + token_count // 2),
         ),
         name="prefill",
-    )(prefix_held, received, prefill_q[0], prefill_new_kv[0])
+    )(prefix_held, *bundles, prefill_q[0], prefill_new_kv[0])
 
     decode_out = pl.pallas_call(
         functools.partial(unpack_kernel, cap, head_rows),

time: 63.7 us -> 64.1 us (level); the launches traced: 63.7 us -> 63.2 us
  waiting for transfers between devices: 21.6 us -> 9.48 us
  starting transfers between devices: 16 us -> 21.3 us
  local copies, waits for them, and re-layouts: 1.29 us -> 4.98 us
  Pallas kernels: 24.2 us -> 26.6 us
    all_to_all x1, waiting for transfers between devices: 17.9 us -> 0.01 us  [shards(): lax.all_to_all(sending, 'pool', split_axis=0, concat_axis=0, tiled=True)]
    ppermute x0 -> x8, starting transfers between devices: none -> 10.2 us  [the longest x7 7.35 us: shards(): lax.ppermute(shares[t], 'pool', [(i, i ^ t) for i in range(devices)])]
    ppermute x0 -> x8, waiting for transfers between devices: none -> 5.88 us  [the longest x7 5.87 us: shards(): lax.ppermute(shares[t], 'pool', [(i, i ^ t) for i in range(devices)])]
    all_to_all x1, starting transfers between devices: 8.63 us -> 3.74 us  [shards(): lax.all_to_all(answers, 'pool', split_axis=0, concat_axis=0, tiled=True)]
    unnamed x12 -> x20, local copies, waits for them, and re-layouts: 1.29 us -> 4.98 us
    pallas_call x1 -> x3, Pallas kernels: 10.8 us -> 13.1 us  [the longest x1 10.8 us: shards(): pl.pallas_call(functools.partial(prefill_kernel, prefill_groups, min(256,...]
    pallas_call x1, Pallas kernels: 5.56 us -> 6.79 us  [shards(): pl.pallas_call(functools.partial(decode_kernel, layout, chunk, width), ou...]
    pallas_call x1, Pallas kernels: 3.3 us -> 2.36 us  [shards(): pl.pallas_call(functools.partial(pack_kernel, layout), out_shape=jax.Shap...]
  transfers between devices with their start and end apart: 2 -> 10, of which waited for: 2 -> 5; matrix products, arithmetic and copies ran while one was open for 0% -> 0% of each run, Pallas kernels for 21% -> 36%
where the time goes in v1:
time: 64.1 us; the launch traced here: 63.2 us
  Pallas kernels  26.6 us (41%)
  starting transfers between devices  21.3 us (33%)
  waiting for transfers between devices  9.48 us (15%)
  local copies, waits for them, and re-layouts  4.98 us (8%)
  between operations  0.76 us (1%)
    pallas_call x1, Pallas kernels, shards(): pl.pallas_call(functools.partial(prefill_kernel, prefill_groups, min(256,...  10.8 us
    all_to_all x1, starting transfers between devices, shards(): lax.all_to_all(sending, 'pool', split_axis=0, concat_axis=0, tiled=True)  7.37 us
    ppermute x7, starting transfers between devices, shards(): lax.ppermute(shares[t], 'pool', [(i, i ^ t) for i in range(devices)])  7.35 us
    pallas_call x1, Pallas kernels, shards(): pl.pallas_call(functools.partial(decode_kernel, layout, chunk, width), ou...  6.79 us
    ppermute x7, waiting for transfers between devices, shards(): lax.ppermute(shares[t], 'pool', [(i, i ^ t) for i in range(devices)])  5.87 us
    unnamed x20, local copies, waits for them, and re-layouts  4.98 us
    all_to_all x1, starting transfers between devices, shards(): lax.all_to_all(answers, 'pool', split_axis=0, concat_axis=0, tiled=True)  3.74 us
    all_to_all x1, waiting for transfers between devices, shards(): lax.all_to_all(answers, 'pool', split_axis=0, concat_axis=0, tiled=True)  3.6 us
  transfers between devices with their start and end apart: 10, of which 5 were waited for; matrix products, arithmetic and copies ran while one was open for 0% of the time, Pallas kernels for 36%

profile of v1, /device:TPU:0, one launch (start us, length us, event | category | flops | bytes accessed | tf_op | source)
XLA Modules:
  0.0 63.2 jit_solution(12927748061889438729)
XLA Ops:
  0.6 0.0 copy-start.8
  0.6 0.0 copy-start.7
  0.7 2.4 %pack.1 = bf16[4,4,160,128]{3,2,1,0:T(8,128)(2,1)} custom-call(s32[256]{0:T(256)} %bitcast.6, bf16[16,8192]{1,0:T(8,128)(2,1)} %q.1, bf16[16,2048]{1,0:T(8,128)(2,1)} %kv.1), custom_call_target="tpu_custom_call" | custom-call | tf_op jit(solution)/shard_map/pack/pallas_call | solution.py:379
  3.0 7.4 %all-to-all-start = ((bf16[16,160,128]{2,1,0:T(8,128)(2,1)}), bf16[16,160,128]{2,1,0:T(8,128)(2,1)S(1)}, u32[]{:S(2)}, u32[]{:S(2)}) async-start(bf16[16,160,128]{2,1,0:T(8,128)(2,1)} %bitcast.12), calls=%async_computation | async-start | bytes 1310720 | tf_op jit(solution)/shard_map/all_to_all | solution.py:395
  10.4 0.0 copy-start
  10.4 0.9 %copy-done = bf16[4,8,16,256]{3,2,1,0:T(8,128)(2,1)S(1)} copy-done((bf16[4,8,16,256]{3,2,1,0:T(8,128)(2,1)S(1)}, bf16[4,8,16,256]{3,2,1,0:T(8,128)(2,1)}, u32[]{:S(2)}) %copy-start) | copy-done | bytes 262168
  11.3 0.0 copy-start.3
  11.4 0.7 %copy-done.3 = s32[2,32]{1,0:T(2,128)S(1)} copy-done((s32[2,32]{1,0:T(2,128)S(1)}, s32[2,32]{1,0:T(2,128)}, u32[]{:S(2)}) %copy-start.3) | copy-done | bytes 280
  12.0 0.0 copy-start.5
  12.0 0.7 %copy-done.5 = s32[2]{0:T(128)S(1)} copy-done((s32[2]{0:T(128)S(1)}, s32[2]{0:T(128)}, u32[]{:S(2)}) %copy-start.5) | copy-done | bytes 32
  12.7 1.7 %blocks.1 = (bf16[2,2,16,256]{3,2,1,0:T(8,128)(2,1)S(1)}, bf16[2,2,16,256]{3,2,1,0:T(8,128)(2,1)S(1)}, bf16[2,2,16,256]{3,2,1,0:T(8,128)(2,1)S(1)}, bf16[2,2,16,...) custom-call(s32[2,32]{1,0:T(2,128)S(1)} %copy-done.3, ...), custom_call_target="tpu_custom_call" | custom-call | flops 100000 | bytes 1000000 | tf_op jit(solution)/shard_map/blocks/pallas_call | solution.py:398
  14.4 0.5 collective-permute-start
  14.9 1.7 %collective-permute-start.1 = (bf16[2,2,16,256]{3,2,1,0:T(8,128)(2,1)S(1)}, bf16[2,2,16,256]{3,2,1,0:T(8,128)(2,1)S(1)}, u32[]{:S(2)}, u32[]{:S(2)}) collective-permute-start(bf16[2,2,16,256]{3,2,1,0:T(8,128)(2,1)S(1)} %get-tuple-element.27), channel_id=1, source_target_pairs={{0,2},{1,3},{2,0},{3,1},{4,6},{5,7},{6,4},{7,5},{8,10},{9,11},{10,... | collective-permute-start | bytes 98312 | tf_op jit(solution)/shard_map/ppermute | solution.py:409
  16.6 0.0 collective-permute-start.2
  16.6 1.7 %collective-permute-start.3 = (bf16[2,2,16,256]{3,2,1,0:T(8,128)(2,1)S(1)}, bf16[2,2,16,256]{3,2,1,0:T(8,128)(2,1)S(1)}, u32[]{:S(2)}, u32[]{:S(2)}) collective-permute-start(bf16[2,2,16,256]{3,2,1,0:T(8,128)(2,1)S(1)} %get-tuple-element.29), channel_id=1, source_target_pairs={{0,4},{1,5},{2,6},{3,7},{4,0},{5,1},{6,2},{7,3},{8,12},{9,13},{10,... | collective-permute-start | bytes 98312 | tf_op jit(solution)/shard_map/ppermute | solution.py:409
  18.3 0.1 collective-permute-start.4
  18.4 0.0 collective-permute-done.rest_1_
  18.4 2.6 %collective-permute-start.5 = (bf16[2,2,16,256]{3,2,1,0:T(8,128)(2,1)S(1)}, bf16[2,2,16,256]{3,2,1,0:T(8,128)(2,1)S(1)}, u32[]{:S(2)}, u32[]{:S(2)}) collective-permute-start(bf16[2,2,16,256]{3,2,1,0:T(8,128)(2,1)S(1)} %get-tuple-element.31), channel_id=1, source_target_pairs={{0,6},{1,7},{2,4},{3,5},{4,2},{5,3},{6,0},{7,1},{8,14},{9,15},{10,... | collective-permute-start | bytes 98312 | tf_op jit(solution)/shard_map/ppermute | solution.py:409
  21.0 0.0 collective-permute-done.1.rest_2_
  21.0 0.8 %collective-permute-start.6 = (bf16[2,2,16,256]{3,2,1,0:T(8,128)(2,1)S(1)}, bf16[2,2,16,256]{3,2,1,0:T(8,128)(2,1)S(1)}, u32[]{:S(2)}, u32[]{:S(2)}) collective-permute-start(bf16[2,2,16,256]{3,2,1,0:T(8,128)(2,1)S(1)} %get-tuple-element.32), channel_id=1, source_target_pairs={{0,7},{1,6},{2,5},{3,4},{4,3},{5,2},{6,1},{7,0},{8,15},{9,14},{10,... | collective-permute-start | bytes 98312 | tf_op jit(solution)/shard_map/ppermute | solution.py:409
  21.8 0.0 collective-permute-done.2.rest_3_
  21.8 1.6 %collective-permute-done.3.rest_4_ = bf16[2,2,16,256]{3,2,1,0:T(8,128)(2,1)S(1)} collective-permute-done((bf16[2,2,16,256]{3,2,1,0:T(8,128)(2,1)S(1)}, bf16[2,2,16,256]{3,2,1,0:T(8,128)(2,1)S(1)}, u32[]{:S(2)}, u32[]{:S(2)}) %collective-permute-start.3) | collective-permute-done | bytes 32800 | tf_op jit(solution)/shard_map/ppermute | solution.py:409
  23.4 0.2 collective-permute-done.4.rest_5_
  23.6 0.8 %collective-permute-done.5.rest_6_ = bf16[2,2,16,256]{3,2,1,0:T(8,128)(2,1)S(1)} collective-permute-done((bf16[2,2,16,256]{3,2,1,0:T(8,128)(2,1)S(1)}, bf16[2,2,16,256]{3,2,1,0:T(8,128)(2,1)S(1)}, u32[]{:S(2)}, u32[]{:S(2)}) %collective-permute-start.5) | collective-permute-done | bytes 32800 | tf_op jit(solution)/shard_map/ppermute | solution.py:409
  24.5 3.2 %collective-permute-done.6.rest_7_ = bf16[2,2,16,256]{3,2,1,0:T(8,128)(2,1)S(1)} collective-permute-done((bf16[2,2,16,256]{3,2,1,0:T(8,128)(2,1)S(1)}, bf16[2,2,16,256]{3,2,1,0:T(8,128)(2,1)S(1)}, u32[]{:S(2)}, u32[]{:S(2)}) %collective-permute-start.6) | collective-permute-done | bytes 32800 | tf_op jit(solution)/shard_map/ppermute | solution.py:409
  27.7 0.0 copy-start.2
  27.7 0.5 regroup.1
  28.2 0.0 all-to-all-done.recv
  28.2 2.8 %collective-permute-start.7 = (bf16[8,2,16,256]{3,2,1,0:T(8,128)(2,1)S(1)}, bf16[8,2,16,256]{3,2,1,0:T(8,128)(2,1)S(1)}, u32[]{:S(2)}, u32[]{:S(2)}) collective-permute-start(bf16[8,2,16,256]{3,2,1,0:T(8,128)(2,1)S(1)} %get-tuple-element.37), channel_id=1, source_target_pairs={{0,8},{1,9},{2,10},{3,11},{4,12},{5,13},{6,14},{7,15},{8,0},{9,1},... | collective-permute-start | bytes 393224 | tf_op jit(solution)/shard_map/ppermute | solution.py:425
  31.0 0.0 copy-start.1
  31.0 0.7 %copy-done.1 = s32[256,1]{0,1:T(1,128)S(1)} copy-done((s32[256,1]{0,1:T(1,128)S(1)}, s32[256,1]{0,1:T(1,128)}, u32[]{:S(2)}) %copy-start.1) | copy-done | bytes 1048
  31.7 0.0 copy-start.4
  31.7 0.7 %copy-done.4 = s32[2,32]{1,0:T(2,128)S(1)} copy-done((s32[2,32]{1,0:T(2,128)S(1)}, s32[2,32]{1,0:T(2,128)}, u32[]{:S(2)}) %copy-start.4) | copy-done | bytes 280
  32.4 0.0 copy-start.6
  32.4 0.7 %copy-done.6 = s32[2]{0:T(128)S(1)} copy-done((s32[2]{0:T(128)S(1)}, s32[2]{0:T(128)}, u32[]{:S(2)}) %copy-start.6) | copy-done | bytes 32
  33.0 0.0 copy-start.9
  33.0 0.7 %copy-done.9 = s32[256]{0:T(256)S(1)} copy-done((s32[256]{0:T(256)S(1)}, s32[256]{0:T(256)}, u32[]{:S(2)}) %copy-start.9) | copy-done | bytes 1048
  33.7 2.8 %plan.1 = (s32[128]{0:T(128)S(1)}, s32[34]{0:T(128)S(1)}, s32[64]{0:T(128)S(1)}) custom-call(s32[2,32]{1,0:T(2,128)S(1)} %copy-done.4, s32[2]{0:T(128)S(1)} %copy-done.6, s32[256]{0:T(256)S(1)} %bitcast.7, s32[256]{0:T(256)S(1)} %copy-done.9), custom_call_target="tpu_custom_call" | custom-call | flops 1000000 | bytes 4000000 | tf_op jit(solution)/shard_map/plan/pallas_call | solution.py:436
  36.5 6.8 %decode.1 = bf16[16,128,128]{2,1,0:T(8,128)(2,1)} custom-call(s32[34]{0:T(128)S(1)} %get-tuple-element.23.listed, s32[128]{0:T(128)S(1)} %get-tuple-element.24.slot_len, bf16[16,160,128]{2,1,0:T(8,128)(2,1)S(1)} %all-to-all-done.recv, bf16[128,2,64,256]{3,2,1,0:T(8,128)(2,1)} %bitcast.11), custom_call_target="tpu_custom_call" | custom-call | flops 500000000 | bytes 8000000 | tf_op jit(solution)/shard_map/decode/pallas_call | solution.py:450
  43.3 0.0 collective-permute-done.7.rest_1_
  43.3 3.7 %all-to-all-start.1 = ((bf16[16,128,128]{2,1,0:T(8,128)(2,1)}), bf16[16,128,128]{2,1,0:T(8,128)(2,1)S(1)}, u32[]{:S(2)}, u32[]{:S(2)}) async-start(bf16[16,128,128]{2,1,0:T(8,128)(2,1)} %decode.1), calls=%async_computation.1 | async-start | bytes 1048576 | tf_op jit(solution)/shard_map/all_to_all | solution.py:467
  47.1 0.0 copy-done.8
  47.1 0.0 copy-done.7
  47.1 10.8 %prefill.1 = bf16[512,1024]{1,0:T(8,128)(2,1)} custom-call(s32[64]{0:T(128)S(1)} %get-tuple-element.39.prefix_held, bf16[8,2,16,256]{3,2,1,0:T(8,128)(2,1)S(1)} %get-tuple-element.40.rest_0_, bf16[8,2,16,256]{3,2,1,0:T(8,128)(2,1)S(1)} %collective-permute-done.7.rest_1_, bf16[512,1024]{1,0:T(8,128)(2,1)S(1)} %bitcast.9, bf16[512,256]{1,0:T(8,128)(2,1)S(1)} %bitcast.10), custom_call_target="tpu_custom_call" | custom-call | flops 1610612736 | bytes 3000000 | tf_op jit(solution)/shard_map/prefill/pallas_call | solution.py:473
  57.9 3.6 %all-to-all-done.1.back = bf16[16,128,128]{2,1,0:T(8,128)(2,1)S(1)} async-done(((bf16[16,128,128]{2,1,0:T(8,128)(2,1)}), bf16[16,128,128]{2,1,0:T(8,128)(2,1)S(1)}, u32[]{:S(2)}, u32[]{:S(2)}) %all-to-all-start.1) | async-done | bytes 524320 | tf_op jit(solution)/shard_map/all_to_all | solution.py:467
  61.5 0.0 copy-done.2
  61.5 1.6 %unpack.1 = bf16[16,8192]{1,0:T(8,128)(2,1)} custom-call(s32[256]{0:T(256)S(1)} %bitcast.8, bf16[16,128,128]{2,1,0:T(8,128)(2,1)S(1)} %all-to-all-done.1.back), custom_call_target="tpu_custom_call" | custom-call | tf_op jit(solution)/shard_map/unpack/pallas_call | solution.py:498
Async XLA Ops:
  0.6 46.4 %copy-start.8 = (bf16[1,512,256]{2,1,0:T(8,128)(2,1)S(1)}, bf16[1,512,256]{2,1,0:T(8,128)(2,1)}, u32[]{:S(2)}) copy-start(bf16[1,512,256]{2,1,0:T(8,128)(2,1)} %param.14) | copy-start | bytes 786436
  0.6 46.4 %copy-start.7 = (bf16[1,512,1024]{2,1,0:T(8,128)(2,1)S(1)}, bf16[1,512,1024]{2,1,0:T(8,128)(2,1)}, u32[]{:S(2)}) copy-start(bf16[1,512,1024]{2,1,0:T(8,128)(2,1)} %param.13) | copy-start | bytes 3145732
  3.0 25.1 %all-to-all-start = ((bf16[16,160,128]{2,1,0:T(8,128)(2,1)}), bf16[16,160,128]{2,1,0:T(8,128)(2,1)S(1)}, u32[]{:S(2)}, u32[]{:S(2)}) async-start(bf16[16,160,128]{2,1,0:T(8,128)(2,1)} %bitcast.12), calls=%async_computation | async-start | bytes 1310720 | tf_op jit(solution)/shard_map/all_to_all | solution.py:395
  10.4 1.0 %copy-start = (bf16[4,8,16,256]{3,2,1,0:T(8,128)(2,1)S(1)}, bf16[4,8,16,256]{3,2,1,0:T(8,128)(2,1)}, u32[]{:S(2)}) copy-start(bf16[4,8,16,256]{3,2,1,0:T(8,128)(2,1)} %pool.1) | copy-start | bytes 786436
  11.3 0.7 %copy-start.3 = (s32[2,32]{1,0:T(2,128)S(1)}, s32[2,32]{1,0:T(2,128)}, u32[]{:S(2)}) copy-start(s32[2,32]{1,0:T(2,128)} %table.3) | copy-start | bytes 772
  12.0 0.7 %copy-start.5 = (s32[2]{0:T(128)S(1)}, s32[2]{0:T(128)}, u32[]{:S(2)}) copy-start(s32[2]{0:T(128)} %count.3) | copy-start | bytes 28
  14.4 4.0 %collective-permute-start = (bf16[2,2,16,256]{3,2,1,0:T(8,128)(2,1)S(1)}, bf16[2,2,16,256]{3,2,1,0:T(8,128)(2,1)S(1)}, u32[]{:S(2)}, u32[]{:S(2)}) collective-permute-start(bf16[2,2,16,256]{3,2,1,0:T(8,128)(2,1)S(1)} %get-tuple-element.26), channel_id=1, source_target_pairs={{0,1},{1,0},{2,3},{3,2},{4,5},{5,4},{6,7},{7,6},{8,9},{9,8},{10,11... | collective-permute-start | bytes 98312 | tf_op jit(solution)/shard_map/ppermute | solution.py:409
  14.9 6.1 %collective-permute-start.1 = (bf16[2,2,16,256]{3,2,1,0:T(8,128)(2,1)S(1)}, bf16[2,2,16,256]{3,2,1,0:T(8,128)(2,1)S(1)}, u32[]{:S(2)}, u32[]{:S(2)}) collective-permute-start(bf16[2,2,16,256]{3,2,1,0:T(8,128)(2,1)S(1)} %get-tuple-element.27), channel_id=1, source_target_pairs={{0,2},{1,3},{2,0},{3,1},{4,6},{5,7},{6,4},{7,5},{8,10},{9,11},{10,... | collective-permute-start | bytes 98312 | tf_op jit(solution)/shard_map/ppermute | solution.py:409
  16.6 5.2 %collective-permute-start.2 = (bf16[2,2,16,256]{3,2,1,0:T(8,128)(2,1)S(1)}, bf16[2,2,16,256]{3,2,1,0:T(8,128)(2,1)S(1)}, u32[]{:S(2)}, u32[]{:S(2)}) collective-permute-start(bf16[2,2,16,256]{3,2,1,0:T(8,128)(2,1)S(1)} %get-tuple-element.28), channel_id=1, source_target_pairs={{0,3},{1,2},{2,1},{3,0},{4,7},{5,6},{6,5},{7,4},{8,11},{9,10},{10,... | collective-permute-start | bytes 98312 | tf_op jit(solution)/shard_map/ppermute | solution.py:409
  16.6 6.8 %collective-permute-start.3 = (bf16[2,2,16,256]{3,2,1,0:T(8,128)(2,1)S(1)}, bf16[2,2,16,256]{3,2,1,0:T(8,128)(2,1)S(1)}, u32[]{:S(2)}, u32[]{:S(2)}) collective-permute-start(bf16[2,2,16,256]{3,2,1,0:T(8,128)(2,1)S(1)} %get-tuple-element.29), channel_id=1, source_target_pairs={{0,4},{1,5},{2,6},{3,7},{4,0},{5,1},{6,2},{7,3},{8,12},{9,13},{10,... | collective-permute-start | bytes 98312 | tf_op jit(solution)/shard_map/ppermute | solution.py:409
  18.3 5.3 %collective-permute-start.4 = (bf16[2,2,16,256]{3,2,1,0:T(8,128)(2,1)S(1)}, bf16[2,2,16,256]{3,2,1,0:T(8,128)(2,1)S(1)}, u32[]{:S(2)}, u32[]{:S(2)}) collective-permute-start(bf16[2,2,16,256]{3,2,1,0:T(8,128)(2,1)S(1)} %get-tuple-element.30), channel_id=1, source_target_pairs={{0,5},{1,4},{2,7},{3,6},{4,1},{5,0},{6,3},{7,2},{8,13},{9,12},{10,... | collective-permute-start | bytes 98312 | tf_op jit(solution)/shard_map/ppermute | solution.py:409
  18.4 6.1 %collective-permute-start.5 = (bf16[2,2,16,256]{3,2,1,0:T(8,128)(2,1)S(1)}, bf16[2,2,16,256]{3,2,1,0:T(8,128)(2,1)S(1)}, u32[]{:S(2)}, u32[]{:S(2)}) collective-permute-start(bf16[2,2,16,256]{3,2,1,0:T(8,128)(2,1)S(1)} %get-tuple-element.31), channel_id=1, source_target_pairs={{0,6},{1,7},{2,4},{3,5},{4,2},{5,3},{6,0},{7,1},{8,14},{9,15},{10,... | collective-permute-start | bytes 98312 | tf_op jit(solution)/shard_map/ppermute | solution.py:409
  21.0 6.7 %collective-permute-start.6 = (bf16[2,2,16,256]{3,2,1,0:T(8,128)(2,1)S(1)}, bf16[2,2,16,256]{3,2,1,0:T(8,128)(2,1)S(1)}, u32[]{:S(2)}, u32[]{:S(2)}) collective-permute-start(bf16[2,2,16,256]{3,2,1,0:T(8,128)(2,1)S(1)} %get-tuple-element.32), channel_id=1, source_target_pairs={{0,7},{1,6},{2,5},{3,4},{4,3},{5,2},{6,1},{7,0},{8,15},{9,14},{10,... | collective-permute-start | bytes 98312 | tf_op jit(solution)/shard_map/ppermute | solution.py:409
  27.7 33.9 %copy-start.2 = (s32[256,1]{0,1:T(1,128)S(1)}, s32[256,1]{0,1:T(1,128)}, u32[]{:S(2)}) copy-start(s32[256,1]{0,1:T(1,128)} %param.18) | copy-start | bytes 3076
  28.2 15.1 %collective-permute-start.7 = (bf16[8,2,16,256]{3,2,1,0:T(8,128)(2,1)S(1)}, bf16[8,2,16,256]{3,2,1,0:T(8,128)(2,1)S(1)}, u32[]{:S(2)}, u32[]{:S(2)}) collective-permute-start(bf16[8,2,16,256]{3,2,1,0:T(8,128)(2,1)S(1)} %get-tuple-element.37), channel_id=1, source_target_pairs={{0,8},{1,9},{2,10},{3,11},{4,12},{5,13},{6,14},{7,15},{8,0},{9,1},... | collective-permute-start | bytes 393224 | tf_op jit(solution)/shard_map/ppermute | solution.py:425
  31.0 0.7 %copy-start.1 = (s32[256,1]{0,1:T(1,128)S(1)}, s32[256,1]{0,1:T(1,128)}, u32[]{:S(2)}) copy-start(s32[256,1]{0,1:T(1,128)} %param.18) | copy-start | bytes 3076
  31.7 0.7 %copy-start.4 = (s32[2,32]{1,0:T(2,128)S(1)}, s32[2,32]{1,0:T(2,128)}, u32[]{:S(2)}) copy-start(s32[2,32]{1,0:T(2,128)} %table.3) | copy-start | bytes 772
  32.4 0.7 %copy-start.6 = (s32[2]{0:T(128)S(1)}, s32[2]{0:T(128)}, u32[]{:S(2)}) copy-start(s32[2]{0:T(128)} %count.3) | copy-start | bytes 28
  33.0 0.7 %copy-start.9 = (s32[256]{0:T(256)S(1)}, s32[256]{0:T(256)}, u32[]{:S(2)}) copy-start(s32[256]{0:T(256)} %lengths.1) | copy-start | bytes 3076
  43.3 18.2 %all-to-all-start.1 = ((bf16[16,128,128]{2,1,0:T(8,128)(2,1)}), bf16[16,128,128]{2,1,0:T(8,128)(2,1)S(1)}, u32[]{:S(2)}, u32[]{:S(2)}) async-start(bf16[16,128,128]{2,1,0:T(8,128)(2,1)} %decode.1), calls=%async_computation.1 | async-start | bytes 1048576 | tf_op jit(solution)/shard_map/all_to_all | solution.py:467

commit v2 on v1

--- a/solution.py
+++ b/solution.py
@@ -10,6 +10,7 @@
 PGRP = 8
 DGRP = 4
 PCAP = 2
+PLANE = 4
 LANES = 128
 MASKED = -1e30
 LOG2E = 1.4426950408889634
@@ -84,7 +85,7 @@
 
 
 def blocks_kernel(table, count, pool, *rest):
-    outs, sems = rest[:PGRP], rest[PGRP]
+    outs, sems = rest[:PLANE], rest[PLANE]
     blocks_here = pool.shape[0]
     group_count, most_blocks = table.shape
     device = lax.axis_index("pool")
@@ -111,7 +112,7 @@
             for k in range(PCAP):
                 copy = pltpu.make_async_copy(
                     pool.at[chosen[k], (device % PGRP) ^ t],
-                    outs[t].at[g, k],
+                    outs[t % PLANE].at[t // PLANE, g, k],
                     sems.at[((g % 2) * PGRP + t) * PCAP + k],
                 )
                 copy.start()
@@ -122,17 +123,30 @@
             copy.wait()
 
 
+def forward_kernel(*rest):
+    held, out, sems = rest[:PLANE], rest[PLANE], rest[PLANE + 1]
+    copies = []
+    for t in range(PLANE):
+        copy = pltpu.make_async_copy(held[t].at[1], out.at[t], sems.at[t])
+        copy.start()
+        copies.append(copy)
+    for copy in copies:
+        copy.wait()
+
+
 def regroup_kernel(group_count, *rest):
-    held, outs, sems = rest[:PGRP], rest[PGRP : PGRP + group_count], rest[-1]
+    held, crossed = rest[:PLANE], rest[PLANE]
+    outs, sems = rest[PLANE + 1 : PLANE + 1 + group_count], rest[-1]
     mine = lax.axis_index("pool") // PGRP
     copies = []
     for x in range(group_count):
-        for t in range(PGRP):
-            copy = pltpu.make_async_copy(
-                held[t].at[(mine + x) % group_count], outs[x].at[t], sems.at[x * PGRP + t]
-            )
-            copy.start()
-            copies.append(copy)
+        g = (mine + x) % group_count
+        for t in range(PLANE):
+            for side, source in enumerate((held[t].at[0, g], crossed.at[t, g])):
+                place = side * PLANE + t
+                copy = pltpu.make_async_copy(source, outs[x].at[place], sems.at[x * PGRP + place])
+                copy.start()
+                copies.append(copy)
     for copy in copies:
         copy.wait()
 
@@ -394,41 +408,45 @@
 
     received = lax.all_to_all(sending, "pool", split_axis=0, concat_axis=0, tiled=True)
 
-    share = jax.ShapeDtypeStruct((prefill_groups, PCAP, blk, 2 * LANES), jnp.bfloat16)
+    share = jax.ShapeDtypeStruct(
+        (PGRP // PLANE, prefill_groups, PCAP, blk, 2 * LANES), jnp.bfloat16
+    )
     shares = pl.pallas_call(
         blocks_kernel,
-        out_shape=(share,) * PGRP,
+        out_shape=(share,) * PLANE,
         in_specs=[smem_spec(), smem_spec(), any_spec()],
-        out_specs=(any_spec(),) * PGRP,
+        out_specs=(any_spec(),) * PLANE,
         scratch_shapes=[pltpu.SemaphoreType.DMA((2 * PGRP * PCAP,))],
-        compiler_params=small,
+        compiler_params=big,
         cost_estimate=pl.CostEstimate(flops=100000, bytes_accessed=1000000, transcendentals=0),
         name="blocks",
     )(prefix_table, prefix_count, pool_kv)
     shares = [shares[0]] + [
         lax.ppermute(shares[t], "pool", [(i, i ^ t) for i in range(devices)])
-        for t in range(1, PGRP)
+        for t in range(1, PLANE)
     ]
+    far_half = pl.pallas_call(
+        forward_kernel,
+        out_shape=jax.ShapeDtypeStruct((PLANE,) + share.shape[1:], jnp.bfloat16),
+        in_specs=[any_spec()] * PLANE,
+        out_specs=any_spec(),
+        scratch_shapes=[pltpu.SemaphoreType.DMA((PLANE,))],
+        compiler_params=small,
+        cost_estimate=pl.CostEstimate(flops=100000, bytes_accessed=1000000, transcendentals=0),
+        name="forward",
+    )(*shares)
+    far_half = lax.ppermute(far_half, "pool", [(i, i ^ PLANE) for i in range(devices)])
     bundle = jax.ShapeDtypeStruct((PGRP, PCAP, blk, 2 * LANES), jnp.bfloat16)
     bundles = pl.pallas_call(
         functools.partial(regroup_kernel, prefill_groups),
         out_shape=(bundle,) * prefill_groups,
-        in_specs=[any_spec()] * PGRP,
+        in_specs=[any_spec()] * (PLANE + 1),
         out_specs=(any_spec(),) * prefill_groups,
         scratch_shapes=[pltpu.SemaphoreType.DMA((prefill_groups * PGRP,))],
         compiler_params=small,
         cost_estimate=pl.CostEstimate(flops=100000, bytes_accessed=1000000, transcendentals=0),
         name="regroup",
-    )(*shares)
-    received, *bundles = lax.optimization_barrier((received, *bundles))
-    bundles = [bundles[0]] + [
-        lax.ppermute(
-            bundles[x],
-            "pool",
-            [(i, (i + x * PGRP) % devices) for i in range(devices)],
-        )
-        for x in range(1, prefill_groups)
-    ]
+    )(*shares, far_half)
 
     chunk = min(cap, 4)
     width = 8
@@ -446,6 +464,18 @@
         cost_estimate=pl.CostEstimate(flops=1000000, bytes_accessed=4000000, transcendentals=0),
         name="plan",
     )(prefix_table, prefix_count, groups, cached_len)
+
+    received, slot_len, listed, *bundles = lax.optimization_barrier(
+        (received, slot_len, listed, *bundles)
+    )
+    bundles = [bundles[0]] + [
+        lax.ppermute(
+            bundles[x],
+            "pool",
+            [(i, (i + x * PGRP) % devices) for i in range(devices)],
+        )
+        for x in range(1, prefill_groups)
+    ]
 
     answers = pl.pallas_call(
         functools.partial(decode_kernel, layout, chunk, width),

time: 64.1 us -> 67.8 us (1.058)
  Pallas kernels: 26.6 us -> 34.1 us
  starting transfers between devices: 21.3 us -> 17.7 us
    pallas_call x1 -> x2, Pallas kernels: 1.73 us -> 10.4 us  [the longest x1 10.2 us: shards(): pl.pallas_call(blocks_kernel, out_shape=(share,) * PLANE, in_specs=[smem_...]
    ppermute x7 -> x3, starting transfers between devices: 7.35 us -> 2.16 us  [shards(): lax.ppermute(shares[t], 'pool', [(i, i ^ t) for i in range(devices)])]
    pallas_call x1, Pallas kernels: 6.79 us -> 5.56 us  [shards(): pl.pallas_call(functools.partial(decode_kernel, layout, chunk, width), ou...]
    ppermute x0 -> x1, starting transfers between devices: none -> 1.06 us  [shards(): lax.ppermute(far_half, 'pool', [(i, i ^ PLANE) for i in range(devices)])]
    ppermute x1, waiting for transfers between devices: 0.01 us -> 0.91 us  [shards(): lax.ppermute(bundles[x], 'pool', [(i, (i + x * PGRP) % devices) for i in...]
    all_to_all x1, starting transfers between devices: 3.74 us -> 4.5 us  [shards(): lax.all_to_all(answers, 'pool', split_axis=0, concat_axis=0, tiled=True)]
    unnamed x20 -> x18, local copies, waits for them, and re-layouts: 4.98 us -> 4.38 us
    ppermute x7 -> x3, waiting for transfers between devices: 5.87 us -> 5.58 us  [shards(): lax.ppermute(shares[t], 'pool', [(i, i ^ t) for i in range(devices)])]
  transfers between devices with their start and end apart: 10 -> 7, of which waited for: 5 -> 4; matrix products, arithmetic and copies ran while one was open for 0% -> 0% of each run, Pallas kernels for 36% -> 45%
where the time goes in v2:
time: 67.8 us; the launch traced here: 67 us
  Pallas kernels  34.1 us (50%)
  starting transfers between devices  17.7 us (26%)
  waiting for transfers between devices  10.1 us (15%)
  local copies, waits for them, and re-layouts  4.38 us (6%)
  between operations  0.77 us (1%)
    pallas_call x1, Pallas kernels, shards(): pl.pallas_call(functools.partial(prefill_kernel, prefill_groups, min(256,...  10.9 us
    pallas_call x1, Pallas kernels, shards(): pl.pallas_call(blocks_kernel, out_shape=(share,) * PLANE, in_specs=[smem_...  10.2 us
    all_to_all x1, starting transfers between devices, shards(): lax.all_to_all(sending, 'pool', split_axis=0, concat_axis=0, tiled=True)  7.37 us
    ppermute x3, waiting for transfers between devices, shards(): lax.ppermute(shares[t], 'pool', [(i, i ^ t) for i in range(devices)])  5.58 us
    pallas_call x1, Pallas kernels, shards(): pl.pallas_call(functools.partial(decode_kernel, layout, chunk, width), ou...  5.56 us
    all_to_all x1, starting transfers between devices, shards(): lax.all_to_all(answers, 'pool', split_axis=0, concat_axis=0, tiled=True)  4.5 us
    unnamed x18, local copies, waits for them, and re-layouts  4.38 us
    all_to_all x1, waiting for transfers between devices, shards(): lax.all_to_all(answers, 'pool', split_axis=0, concat_axis=0, tiled=True)  3.59 us
  transfers between devices with their start and end apart: 7, of which 4 were waited for; matrix products, arithmetic and copies ran while one was open for 0% of the time, Pallas kernels for 45%

profile of v2, /device:TPU:0, one launch (start us, length us, event | category | flops | bytes accessed | tf_op | source)
XLA Modules:
  0.0 67.0 jit_solution(2993446359652345588)
XLA Ops:
  0.6 0.0 copy-start.7
  0.6 0.0 copy-start.6
  0.7 2.4 %pack.1 = bf16[4,4,160,128]{3,2,1,0:T(8,128)(2,1)} custom-call(s32[256]{0:T(256)} %bitcast.6, bf16[16,8192]{1,0:T(8,128)(2,1)} %q.1, bf16[16,2048]{1,0:T(8,128)(2,1)} %kv.1), custom_call_target="tpu_custom_call" | custom-call | tf_op jit(solution)/shard_map/pack/pallas_call | solution.py:393
  3.0 7.4 %all-to-all-start = ((bf16[16,160,128]{2,1,0:T(8,128)(2,1)}), bf16[16,160,128]{2,1,0:T(8,128)(2,1)S(1)}, u32[]{:S(2)}, u32[]{:S(2)}) async-start(bf16[16,160,128]{2,1,0:T(8,128)(2,1)} %bitcast.12), calls=%async_computation | async-start | bytes 1310720 | tf_op jit(solution)/shard_map/all_to_all | solution.py:409
  10.4 10.2 %blocks.1 = (bf16[2,2,2,16,256]{4,3,2,1,0:T(8,128)(2,1)}, bf16[2,2,2,16,256]{4,3,2,1,0:T(8,128)(2,1)}, bf16[2,2,2,16,256]{4,3,2,1,0:T(8,128)(2,1)}, bf16[2,2,2,16,256]{4,3,2,1,0:T(8,128)(2,1)}) custom-call(s32[2,32]{1,0:T(2,128)} %table.3, s32[2]{0:T(128)} %count.3, bf16[4,8,16,256]{3,2,1,0:T(8,128)(2,1)} %pool.1), custom_call_target="tpu_custom_call" | custom-call | flops 100000 | bytes 1000000 | tf_op jit(solution)/shard_map/blocks/pallas_call | solution.py:414
  20.6 0.5 collective-permute-start
  21.1 1.7 %collective-permute-start.1 = (bf16[2,2,2,16,256]{4,3,2,1,0:T(8,128)(2,1)}, bf16[2,2,2,16,256]{4,3,2,1,0:T(8,128)(2,1)S(1)}, u32[]{:S(2)}, u32[]{:S(2)}) collective-permute-start(bf16[2,2,2,16,256]{4,3,2,1,0:T(8,128)(2,1)} %get-tuple-element.25), channel_id=1, source_target_pairs={{0,2},{1,3},{2,0},{3,1},{4,6},{5,7},{6,4},{7,5},{8,10},{9,11},{10,... | collective-permute-start | bytes 196616 | tf_op jit(solution)/shard_map/ppermute | solution.py:425
  22.8 0.0 collective-permute-start.2
  22.8 0.0 collective-permute-done.rest_1_
  22.8 4.9 %collective-permute-done.1.rest_2_ = bf16[2,2,2,16,256]{4,3,2,1,0:T(8,128)(2,1)S(1)} collective-permute-done((bf16[2,2,2,16,256]{4,3,2,1,0:T(8,128)(2,1)}, bf16[2,2,2,16,256]{4,3,2,1,0:T(8,128)(2,1)S(1)}, u32[]{:S(2)}, u32[]{:S(2)}) %collective-permute-start.1) | collective-permute-done | bytes 65568 | tf_op jit(solution)/shard_map/ppermute | solution.py:425
  27.7 0.7 collective-permute-done.2.rest_3_
  28.4 0.0 copy-start
  28.4 0.8 %copy-done = bf16[2,2,2,16,256]{4,3,2,1,0:T(8,128)(2,1)S(1)} copy-done((bf16[2,2,2,16,256]{4,3,2,1,0:T(8,128)(2,1)S(1)}, bf16[2,2,2,16,256]{4,3,2,1,0:T(8,128)(2,1)}, u32[]{:S(2)}) %copy-start) | copy-done | bytes 65560
  29.2 0.2 forward.1
  29.4 1.1 %collective-permute-start.3 = (bf16[4,2,2,16,256]{4,3,2,1,0:T(8,128)(2,1)S(1)}, bf16[4,2,2,16,256]{4,3,2,1,0:T(8,128)(2,1)S(1)}, u32[]{:S(2)}, u32[]{:S(2)}) collective-permute-start(bf16[4,2,2,16,256]{4,3,2,1,0:T(8,128)(2,1)S(1)} %forward.1), channel_id=1, source_target_pairs={{0,4},{1,5},{2,6},{3,7},{4,0},{5,1},{6,2},{7,3},{8,12},{9,13},{10,... | collective-permute-start | bytes 393224 | tf_op jit(solution)/shard_map/ppermute | solution.py:438
  30.5 0.0 copy-start.2
  30.5 0.7 %copy-done.2 = s32[256,1]{0,1:T(1,128)S(1)} copy-done((s32[256,1]{0,1:T(1,128)S(1)}, s32[256,1]{0,1:T(1,128)}, u32[]{:S(2)}) %copy-start.2) | copy-done | bytes 1048
  31.1 0.0 copy-start.4
  31.1 0.7 %copy-done.4 = s32[2,32]{1,0:T(2,128)S(1)} copy-done((s32[2,32]{1,0:T(2,128)S(1)}, s32[2,32]{1,0:T(2,128)}, u32[]{:S(2)}) %copy-start.4) | copy-done | bytes 280
  31.8 0.0 copy-start.5
  31.8 0.7 copy-done.5
  32.5 0.0 copy-start.8
  32.5 0.7 %copy-done.8 = s32[256]{0:T(256)S(1)} copy-done((s32[256]{0:T(256)S(1)}, s32[256]{0:T(256)}, u32[]{:S(2)}) %copy-start.8) | copy-done | bytes 1048
  33.1 2.8 %plan.1 = (s32[128]{0:T(128)S(1)}, s32[34]{0:T(128)S(1)}, s32[64]{0:T(128)S(1)}) custom-call(s32[2,32]{1,0:T(2,128)S(1)} %copy-done.4, s32[2]{0:T(128)S(1)} %copy-done.5, s32[256]{0:T(256)S(1)} %bitcast.7, s32[256]{0:T(256)S(1)} %copy-done.8), custom_call_target="tpu_custom_call" | custom-call | flops 1000000 | bytes 4000000 | tf_op jit(solution)/shard_map/plan/pallas_call | solution.py:454
  35.9 0.0 collective-permute-done.3.rest_4_
  35.9 0.0 copy-start.1
  36.0 0.8 %copy-done.1 = bf16[2,2,2,16,256]{4,3,2,1,0:T(8,128)(2,1)S(1)} copy-done((bf16[2,2,2,16,256]{4,3,2,1,0:T(8,128)(2,1)S(1)}, bf16[2,2,2,16,256]{4,3,2,1,0:T(8,128)(2,1)}, u32[]{:S(2)}) %copy-start.1) | copy-done | bytes 65560
  36.8 0.5 regroup.1
  37.3 0.0 copy-start.3
  37.3 0.0 all-to-all-done.recv
  37.3 2.6 %collective-permute-start.4 = (bf16[8,2,16,256]{3,2,1,0:T(8,128)(2,1)S(1)}, bf16[8,2,16,256]{3,2,1,0:T(8,128)(2,1)S(1)}, u32[]{:S(2)}, u32[]{:S(2)}) collective-permute-start(bf16[8,2,16,256]{3,2,1,0:T(8,128)(2,1)S(1)} %get-tuple-element.33), channel_id=1, source_target_pairs={{0,8},{1,9},{2,10},{3,11},{4,12},{5,13},{6,14},{7,15},{8,0},{9,1},... | collective-permute-start | bytes 393224 | tf_op jit(solution)/shard_map/ppermute | solution.py:472
  39.9 5.6 %decode.1 = bf16[16,128,128]{2,1,0:T(8,128)(2,1)} custom-call(s32[34]{0:T(128)S(1)} %get-tuple-element.29.listed, s32[128]{0:T(128)S(1)} %get-tuple-element.30.slot_len, bf16[16,160,128]{2,1,0:T(8,128)(2,1)S(1)} %all-to-all-done.recv, bf16[128,2,64,256]{3,2,1,0:T(8,128)(2,1)} %bitcast.11), custom_call_target="tpu_custom_call" | custom-call | flops 500000000 | bytes 8000000 | tf_op jit(solution)/shard_map/decode/pallas_call | solution.py:480
  45.5 0.9 %collective-permute-done.4.rest_1_ = bf16[8,2,16,256]{3,2,1,0:T(8,128)(2,1)S(1)} collective-permute-done((bf16[8,2,16,256]{3,2,1,0:T(8,128)(2,1)S(1)}, bf16[8,2,16,256]{3,2,1,0:T(8,128)(2,1)S(1)}, u32[]{:S(2)}, u32[]{:S(2)}) %collective-permute-start.4) | collective-permute-done | bytes 131104 | tf_op jit(solution)/shard_map/ppermute | solution.py:472
  46.4 4.5 %all-to-all-start.1 = ((bf16[16,128,128]{2,1,0:T(8,128)(2,1)}), bf16[16,128,128]{2,1,0:T(8,128)(2,1)S(1)}, u32[]{:S(2)}, u32[]{:S(2)}) async-start(bf16[16,128,128]{2,1,0:T(8,128)(2,1)} %decode.1), calls=%async_computation.1 | async-start | bytes 1048576 | tf_op jit(solution)/shard_map/all_to_all | solution.py:497
  50.9 0.0 copy-done.7
  50.9 0.0 copy-done.6
  50.9 10.9 %prefill.1 = bf16[512,1024]{1,0:T(8,128)(2,1)} custom-call(s32[64]{0:T(128)S(1)} %get-tuple-element.35.prefix_held, bf16[8,2,16,256]{3,2,1,0:T(8,128)(2,1)S(1)} %get-tuple-element.36.rest_0_, bf16[8,2,16,256]{3,2,1,0:T(8,128)(2,1)S(1)} %collective-permute-done.4.rest_1_, bf16[512,1024]{1,0:T(8,128)(2,1)S(1)} %bitcast.9, bf16[512,256]{1,0:T(8,128)(2,1)S(1)} %bitcast.10), custom_call_target="tpu_custom_call" | custom-call | flops 1610612736 | bytes 3000000 | tf_op jit(solution)/shard_map/prefill/pallas_call | solution.py:503
  61.8 3.6 %all-to-all-done.1.back = bf16[16,128,128]{2,1,0:T(8,128)(2,1)S(1)} async-done(((bf16[16,128,128]{2,1,0:T(8,128)(2,1)}), bf16[16,128,128]{2,1,0:T(8,128)(2,1)S(1)}, u32[]{:S(2)}, u32[]{:S(2)}) %all-to-all-start.1) | async-done | bytes 524320 | tf_op jit(solution)/shard_map/all_to_all | solution.py:497
  65.4 0.0 copy-done.3
  65.4 1.6 %unpack.1 = bf16[16,8192]{1,0:T(8,128)(2,1)} custom-call(s32[256]{0:T(256)S(1)} %bitcast.8, bf16[16,128,128]{2,1,0:T(8,128)(2,1)S(1)} %all-to-all-done.1.back), custom_call_target="tpu_custom_call" | custom-call | tf_op jit(solution)/shard_map/unpack/pallas_call | solution.py:528
Async XLA Ops:
  0.6 50.3 %copy-start.7 = (bf16[1,512,256]{2,1,0:T(8,128)(2,1)S(1)}, bf16[1,512,256]{2,1,0:T(8,128)(2,1)}, u32[]{:S(2)}) copy-start(bf16[1,512,256]{2,1,0:T(8,128)(2,1)} %param.14) | copy-start | bytes 786436
  0.6 50.3 %copy-start.6 = (bf16[1,512,1024]{2,1,0:T(8,128)(2,1)S(1)}, bf16[1,512,1024]{2,1,0:T(8,128)(2,1)}, u32[]{:S(2)}) copy-start(bf16[1,512,1024]{2,1,0:T(8,128)(2,1)} %param.13) | copy-start | bytes 3145732
  3.0 34.3 %all-to-all-start = ((bf16[16,160,128]{2,1,0:T(8,128)(2,1)}), bf16[16,160,128]{2,1,0:T(8,128)(2,1)S(1)}, u32[]{:S(2)}, u32[]{:S(2)}) async-start(bf16[16,160,128]{2,1,0:T(8,128)(2,1)} %bitcast.12), calls=%async_computation | async-start | bytes 1310720 | tf_op jit(solution)/shard_map/all_to_all | solution.py:409
  20.6 2.2 %collective-permute-start = (bf16[2,2,2,16,256]{4,3,2,1,0:T(8,128)(2,1)}, bf16[2,2,2,16,256]{4,3,2,1,0:T(8,128)(2,1)S(1)}, u32[]{:S(2)}, u32[]{:S(2)}) collective-permute-start(bf16[2,2,2,16,256]{4,3,2,1,0:T(8,128)(2,1)} %get-tuple-element.24), channel_id=1, source_target_pairs={{0,1},{1,0},{2,3},{3,2},{4,5},{5,4},{6,7},{7,6},{8,9},{9,8},{10,11... | collective-permute-start | bytes 196616 | tf_op jit(solution)/shard_map/ppermute | solution.py:425
  21.1 6.6 %collective-permute-start.1 = (bf16[2,2,2,16,256]{4,3,2,1,0:T(8,128)(2,1)}, bf16[2,2,2,16,256]{4,3,2,1,0:T(8,128)(2,1)S(1)}, u32[]{:S(2)}, u32[]{:S(2)}) collective-permute-start(bf16[2,2,2,16,256]{4,3,2,1,0:T(8,128)(2,1)} %get-tuple-element.25), channel_id=1, source_target_pairs={{0,2},{1,3},{2,0},{3,1},{4,6},{5,7},{6,4},{7,5},{8,10},{9,11},{10,... | collective-permute-start | bytes 196616 | tf_op jit(solution)/shard_map/ppermute | solution.py:425
  22.8 5.6 %collective-permute-start.2 = (bf16[2,2,2,16,256]{4,3,2,1,0:T(8,128)(2,1)}, bf16[2,2,2,16,256]{4,3,2,1,0:T(8,128)(2,1)S(1)}, u32[]{:S(2)}, u32[]{:S(2)}) collective-permute-start(bf16[2,2,2,16,256]{4,3,2,1,0:T(8,128)(2,1)} %get-tuple-element.26), channel_id=1, source_target_pairs={{0,3},{1,2},{2,1},{3,0},{4,7},{5,6},{6,5},{7,4},{8,11},{9,10},{10,... | collective-permute-start | bytes 196616 | tf_op jit(solution)/shard_map/ppermute | solution.py:425
  28.4 0.8 %copy-start = (bf16[2,2,2,16,256]{4,3,2,1,0:T(8,128)(2,1)S(1)}, bf16[2,2,2,16,256]{4,3,2,1,0:T(8,128)(2,1)}, u32[]{:S(2)}) copy-start(bf16[2,2,2,16,256]{4,3,2,1,0:T(8,128)(2,1)} %get-tuple-element.23.rest_0_) | copy-start | bytes 196612
  29.4 6.5 %collective-permute-start.3 = (bf16[4,2,2,16,256]{4,3,2,1,0:T(8,128)(2,1)S(1)}, bf16[4,2,2,16,256]{4,3,2,1,0:T(8,128)(2,1)S(1)}, u32[]{:S(2)}, u32[]{:S(2)}) collective-permute-start(bf16[4,2,2,16,256]{4,3,2,1,0:T(8,128)(2,1)S(1)} %forward.1), channel_id=1, source_target_pairs={{0,4},{1,5},{2,6},{3,7},{4,0},{5,1},{6,2},{7,3},{8,12},{9,13},{10,... | collective-permute-start | bytes 393224 | tf_op jit(solution)/shard_map/ppermute | solution.py:438
  30.5 0.7 %copy-start.2 = (s32[256,1]{0,1:T(1,128)S(1)}, s32[256,1]{0,1:T(1,128)}, u32[]{:S(2)}) copy-start(s32[256,1]{0,1:T(1,128)} %param.18) | copy-start | bytes 3076
  31.1 0.7 %copy-start.4 = (s32[2,32]{1,0:T(2,128)S(1)}, s32[2,32]{1,0:T(2,128)}, u32[]{:S(2)}) copy-start(s32[2,32]{1,0:T(2,128)} %table.3) | copy-start | bytes 772
  31.8 0.7 copy-start.5
  32.5 0.7 %copy-start.8 = (s32[256]{0:T(256)S(1)}, s32[256]{0:T(256)}, u32[]{:S(2)}) copy-start(s32[256]{0:T(256)} %lengths.1) | copy-start | bytes 3076
  35.9 0.8 %copy-start.1 = (bf16[2,2,2,16,256]{4,3,2,1,0:T(8,128)(2,1)S(1)}, bf16[2,2,2,16,256]{4,3,2,1,0:T(8,128)(2,1)}, u32[]{:S(2)}) copy-start(bf16[2,2,2,16,256]{4,3,2,1,0:T(8,128)(2,1)} %get-tuple-element.23.rest_0_) | copy-start | bytes 196612
  37.3 28.1 %copy-start.3 = (s32[256,1]{0,1:T(1,128)S(1)}, s32[256,1]{0,1:T(1,128)}, u32[]{:S(2)}) copy-start(s32[256,1]{0,1:T(1,128)} %param.18) | copy-start | bytes 3076
  37.3 9.1 %collective-permute-start.4 = (bf16[8,2,16,256]{3,2,1,0:T(8,128)(2,1)S(1)}, bf16[8,2,16,256]{3,2,1,0:T(8,128)(2,1)S(1)}, u32[]{:S(2)}, u32[]{:S(2)}) collective-permute-start(bf16[8,2,16,256]{3,2,1,0:T(8,128)(2,1)S(1)} %get-tuple-element.33), channel_id=1, source_target_pairs={{0,8},{1,9},{2,10},{3,11},{4,12},{5,13},{6,14},{7,15},{8,0},{9,1},... | collective-permute-start | bytes 393224 | tf_op jit(solution)/shard_map/ppermute | solution.py:472
  46.4 19.0 %all-to-all-start.1 = ((bf16[16,128,128]{2,1,0:T(8,128)(2,1)}), bf16[16,128,128]{2,1,0:T(8,128)(2,1)S(1)}, u32[]{:S(2)}, u32[]{:S(2)}) async-start(bf16[16,128,128]{2,1,0:T(8,128)(2,1)} %decode.1), calls=%async_computation.1 | async-start | bytes 1048576 | tf_op jit(solution)/shard_map/all_to_all | solution.py:497

commit v3 on v2

--- a/solution.py
+++ b/solution.py
@@ -26,6 +26,10 @@
 
 def smem_spec():
     return pl.BlockSpec(memory_space=pltpu.SMEM)
+
+
+def in_hbm(x):
+    return pltpu.with_memory_space_constraint(x, pltpu.HBM)
 
 
 def vmem_spec():
@@ -387,7 +391,6 @@
     groups = decode_group.reshape(-1)
     prefill_groups = prefix_table.shape[0]
     big = pltpu.CompilerParams(vmem_limit_bytes=60 * 2**20)
-    part = pltpu.CompilerParams(vmem_limit_bytes=52 * 2**20)
     small = pltpu.CompilerParams(vmem_limit_bytes=8 * 2**20)
 
     sending = pl.pallas_call(
@@ -403,7 +406,7 @@
         ],
         compiler_params=big,
         name="pack",
-    )(groups, decode_q, decode_new)
+    )(in_hbm(groups), in_hbm(decode_q), in_hbm(decode_new))
     sending = sending.reshape(devices, message_rows, LANES)
 
     received = lax.all_to_all(sending, "pool", split_axis=0, concat_axis=0, tiled=True)
@@ -417,10 +420,10 @@
         in_specs=[smem_spec(), smem_spec(), any_spec()],
         out_specs=(any_spec(),) * PLANE,
         scratch_shapes=[pltpu.SemaphoreType.DMA((2 * PGRP * PCAP,))],
-        compiler_params=big,
+        compiler_params=small,
         cost_estimate=pl.CostEstimate(flops=100000, bytes_accessed=1000000, transcendentals=0),
         name="blocks",
-    )(prefix_table, prefix_count, pool_kv)
+    )(in_hbm(prefix_table), in_hbm(prefix_count), in_hbm(pool_kv))
     shares = [shares[0]] + [
         lax.ppermute(shares[t], "pool", [(i, i ^ t) for i in range(devices)])
         for t in range(1, PLANE)
@@ -463,7 +466,7 @@
         compiler_params=small,
         cost_estimate=pl.CostEstimate(flops=1000000, bytes_accessed=4000000, transcendentals=0),
         name="plan",
-    )(prefix_table, prefix_count, groups, cached_len)
+    )(in_hbm(prefix_table), in_hbm(prefix_count), in_hbm(groups), in_hbm(cached_len))
 
     received, slot_len, listed, *bundles = lax.optimization_barrier(
         (received, slot_len, listed, *bundles)
@@ -486,12 +489,12 @@
             pltpu.VMEM((block_count * chunk,) + decode_cache.shape[2:], jnp.bfloat16),
             pltpu.SemaphoreType.DMA((block_count,)),
         ],
-        compiler_params=part,
+        compiler_params=pltpu.CompilerParams(vmem_limit_bytes=20 * 2**20),
         cost_estimate=pl.CostEstimate(
             flops=500000000, bytes_accessed=8000000, transcendentals=1000000
         ),
         name="decode",
-    )(listed, slot_len, received, decode_cache[0])
+    )(listed, slot_len, received, in_hbm(decode_cache[0]))
 
     answers, *bundles = lax.optimization_barrier((answers, *bundles))
     back = lax.all_to_all(answers, "pool", split_axis=0, concat_axis=0, tiled=True)
@@ -536,7 +539,7 @@
         ],
         compiler_params=small,
         name="unpack",
-    )(groups, back)
+    )(in_hbm(groups), back)
     return (prefill_out[None], decode_out)
 
 

time: 67.8 us -> 59.8 us (0.88)
  Pallas kernels: 34.1 us -> 27.6 us
  local copies, waits for them, and re-layouts: 4.38 us -> 0.01 us
  waiting for transfers between devices: 10.1 us -> 13.2 us
    pallas_call x1, Pallas kernels: 10.2 us -> 2.29 us  [shards(): pl.pallas_call(blocks_kernel, out_shape=(share,) * PLANE, in_specs=[smem_...]
    unnamed x18 -> x4, local copies, waits for them, and re-layouts: 4.38 us -> 0.01 us
    ppermute x1, waiting for transfers between devices: 0.01 us -> 3.07 us  [shards(): lax.ppermute(far_half, 'pool', [(i, i ^ PLANE) for i in range(devices)])]
    pallas_call x1, Pallas kernels: 5.56 us -> 6.78 us  [shards(): pl.pallas_call(functools.partial(decode_kernel, layout, chunk, width), ou...]
    ppermute x3, waiting for transfers between devices: 5.58 us -> 6.45 us  [shards(): lax.ppermute(shares[t], 'pool', [(i, i ^ t) for i in range(devices)])]
    ppermute x1, waiting for transfers between devices: 0.91 us -> 0.13 us  [shards(): lax.ppermute(bundles[x], 'pool', [(i, (i + x * PGRP) % devices) for i in...]
    ppermute x1, starting transfers between devices: 2.59 us -> 1.84 us  [shards(): lax.ppermute(bundles[x], 'pool', [(i, (i + x * PGRP) % devices) for i in...]
  transfers between devices with their start and end apart: 7 -> 7, of which waited for: 4 -> 5; matrix products, arithmetic and copies ran while one was open for 0% -> 0% of each run, Pallas kernels for 45% -> 40%
where the time goes in v3:
time: 59.8 us; the launch traced here: 59 us
  Pallas kernels  27.6 us (46%)
  starting transfers between devices  17.4 us (29%)
  waiting for transfers between devices  13.2 us (22%)
  between operations  0.74 us (1%)
    pallas_call x1, Pallas kernels, shards(): pl.pallas_call(functools.partial(prefill_kernel, prefill_groups, min(256,...  10.9 us
    all_to_all x1, starting transfers between devices, shards(): lax.all_to_all(sending, 'pool', split_axis=0, concat_axis=0, tiled=True)  7.37 us
    pallas_call x1, Pallas kernels, shards(): pl.pallas_call(functools.partial(decode_kernel, layout, chunk, width), ou...  6.78 us
    ppermute x3, waiting for transfers between devices, shards(): lax.ppermute(shares[t], 'pool', [(i, i ^ t) for i in range(devices)])  6.45 us
    all_to_all x1, starting transfers between devices, shards(): lax.all_to_all(answers, 'pool', split_axis=0, concat_axis=0, tiled=True)  4.67 us
    all_to_all x1, waiting for transfers between devices, shards(): lax.all_to_all(answers, 'pool', split_axis=0, concat_axis=0, tiled=True)  3.6 us
    ppermute x1, waiting for transfers between devices, shards(): lax.ppermute(far_half, 'pool', [(i, i ^ PLANE) for i in range(devices)])  3.07 us
    pallas_call x1, Pallas kernels, shards(): pl.pallas_call(functools.partial(plan_kernel, cap, chunk, devices), out_s...  2.94 us
  transfers between devices with their start and end apart: 7, of which 5 were waited for; matrix products, arithmetic and copies ran while one was open for 0% of the time, Pallas kernels for 40%

profile of v3, /device:TPU:0, one launch (start us, length us, event | category | flops | bytes accessed | tf_op | source)
XLA Modules:
  0.0 59.0 jit_solution(14863045705852981471)
XLA Ops:
  0.6 0.0 copy-start.1
  0.6 0.0 copy-start
  0.7 2.4 %pack.1 = bf16[4,4,160,128]{3,2,1,0:T(8,128)(2,1)} custom-call(s32[256]{0:T(256)} %bitcast.10, bf16[16,8192]{1,0:T(8,128)(2,1)} %q.1, bf16[16,2048]{1,0:T(8,128)(2,1)} %kv.1), custom_call_target="tpu_custom_call" | custom-call | tf_op jit(solution)/shard_map/pack/pallas_call | solution.py:396
  3.0 7.4 %all-to-all-start = ((bf16[16,160,128]{2,1,0:T(8,128)(2,1)}), bf16[16,160,128]{2,1,0:T(8,128)(2,1)S(1)}, u32[]{:S(2)}, u32[]{:S(2)}) async-start(bf16[16,160,128]{2,1,0:T(8,128)(2,1)} %bitcast.9), calls=%async_computation | async-start | bytes 1310720 | tf_op jit(solution)/shard_map/all_to_all | solution.py:412
  10.4 2.3 %blocks.1 = (bf16[2,2,2,16,256]{4,3,2,1,0:T(8,128)(2,1)S(1)}, bf16[2,2,2,16,256]{4,3,2,1,0:T(8,128)(2,1)S(1)}, bf16[2,2,2,16,256]{4,3,2,1,0:T(8,128)(2,1)S(1)}, bf16[2,2,2,16,256]{4,3,2,1,0:T(8,128)(2,1)S(1)}) custom-call(s32[2,32]{1,0:T(2,128)} %table.3, s32[2]{0:T(128)} %count.3, bf16[4,8,16,256]{3,2,1,0:T(8,128)(2,1)} %pool.1), custom_call_target="tpu_custom_call" | custom-call | flops 100000 | bytes 1000000 | tf_op jit(solution)/shard_map/blocks/pallas_call | solution.py:417
  12.7 0.5 collective-permute-start
  13.2 1.7 %collective-permute-start.1 = (bf16[2,2,2,16,256]{4,3,2,1,0:T(8,128)(2,1)S(1)}, bf16[2,2,2,16,256]{4,3,2,1,0:T(8,128)(2,1)S(1)}, u32[]{:S(2)}, u32[]{:S(2)}) collective-permute-start(bf16[2,2,2,16,256]{4,3,2,1,0:T(8,128)(2,1)S(1)} %get-tuple-element.25), channel_id=1, source_target_pairs={{0,2},{1,3},{2,0},{3,1},{4,6},{5,7},{6,4},{7,5},{8,10},{9,11},{10,... | collective-permute-start | bytes 196616 | tf_op jit(solution)/shard_map/ppermute | solution.py:428
  14.8 0.0 collective-permute-start.2
  14.8 0.0 collective-permute-done.rest_1_
  14.9 4.7 %collective-permute-done.1.rest_2_ = bf16[2,2,2,16,256]{4,3,2,1,0:T(8,128)(2,1)S(1)} collective-permute-done((bf16[2,2,2,16,256]{4,3,2,1,0:T(8,128)(2,1)S(1)}, bf16[2,2,2,16,256]{4,3,2,1,0:T(8,128)(2,1)S(1)}, u32[]{:S(2)}, u32[]{:S(2)}) %collective-permute-start.1) | collective-permute-done | bytes 65568 | tf_op jit(solution)/shard_map/ppermute | solution.py:428
  19.6 1.7 %collective-permute-done.2.rest_3_ = bf16[2,2,2,16,256]{4,3,2,1,0:T(8,128)(2,1)S(1)} collective-permute-done((bf16[2,2,2,16,256]{4,3,2,1,0:T(8,128)(2,1)S(1)}, bf16[2,2,2,16,256]{4,3,2,1,0:T(8,128)(2,1)S(1)}, u32[]{:S(2)}, u32[]{:S(2)}) %collective-permute-start.2) | collective-permute-done | bytes 65568 | tf_op jit(solution)/shard_map/ppermute | solution.py:428
  21.3 0.2 forward.1
  21.5 1.3 %collective-permute-start.3 = (bf16[4,2,2,16,256]{4,3,2,1,0:T(8,128)(2,1)S(1)}, bf16[4,2,2,16,256]{4,3,2,1,0:T(8,128)(2,1)S(1)}, u32[]{:S(2)}, u32[]{:S(2)}) collective-permute-start(bf16[4,2,2,16,256]{4,3,2,1,0:T(8,128)(2,1)S(1)} %forward.1), channel_id=1, source_target_pairs={{0,4},{1,5},{2,6},{3,7},{4,0},{5,1},{6,2},{7,3},{8,12},{9,13},{10,... | collective-permute-start | bytes 393224 | tf_op jit(solution)/shard_map/ppermute | solution.py:441
  22.8 2.9 %plan.1 = (s32[128]{0:T(128)S(1)}, s32[34]{0:T(128)S(1)}, s32[64]{0:T(128)S(1)}) custom-call(s32[2,32]{1,0:T(2,128)} %table.3, s32[2]{0:T(128)} %count.3, s32[256]{0:T(256)} %bitcast.11, s32[256]{0:T(256)} %lengths.1), custom_call_target="tpu_custom_call" | custom-call | flops 1000000 | bytes 4000000 | tf_op jit(solution)/shard_map/plan/pallas_call | solution.py:457
  25.8 3.1 %collective-permute-done.3.rest_4_ = bf16[4,2,2,16,256]{4,3,2,1,0:T(8,128)(2,1)S(1)} collective-permute-done((bf16[4,2,2,16,256]{4,3,2,1,0:T(8,128)(2,1)S(1)}, bf16[4,2,2,16,256]{4,3,2,1,0:T(8,128)(2,1)S(1)}, u32[]{:S(2)}, u32[]{:S(2)}) %collective-permute-start.3) | collective-permute-done | bytes 131104 | tf_op jit(solution)/shard_map/ppermute | solution.py:441
  28.8 0.5 regroup.1
  29.3 0.0 all-to-all-done.recv
  29.3 1.8 %collective-permute-start.4 = (bf16[8,2,16,256]{3,2,1,0:T(8,128)(2,1)S(1)}, bf16[8,2,16,256]{3,2,1,0:T(8,128)(2,1)S(1)}, u32[]{:S(2)}, u32[]{:S(2)}) collective-permute-start(bf16[8,2,16,256]{3,2,1,0:T(8,128)(2,1)S(1)} %get-tuple-element.33), channel_id=1, source_target_pairs={{0,8},{1,9},{2,10},{3,11},{4,12},{5,13},{6,14},{7,15},{8,0},{9,1},... | collective-permute-start | bytes 393224 | tf_op jit(solution)/shard_map/ppermute | solution.py:475
  31.2 6.8 %decode.1 = bf16[16,128,128]{2,1,0:T(8,128)(2,1)} custom-call(s32[34]{0:T(128)S(1)} %get-tuple-element.29.listed, s32[128]{0:T(128)S(1)} %get-tuple-element.30.slot_len, bf16[16,160,128]{2,1,0:T(8,128)(2,1)S(1)} %all-to-all-done.recv, bf16[128,2,64,256]{3,2,1,0:T(8,128)(2,1)} %bitcast.8), custom_call_target="tpu_custom_call" | custom-call | flops 500000000 | bytes 8000000 | tf_op jit(solution)/shard_map/decode/pallas_call | solution.py:483
  38.0 0.1 collective-permute-done.4.rest_1_
  38.1 4.7 %all-to-all-start.1 = ((bf16[16,128,128]{2,1,0:T(8,128)(2,1)}), bf16[16,128,128]{2,1,0:T(8,128)(2,1)S(1)}, u32[]{:S(2)}, u32[]{:S(2)}) async-start(bf16[16,128,128]{2,1,0:T(8,128)(2,1)} %decode.1), calls=%async_computation.1 | async-start | bytes 1048576 | tf_op jit(solution)/shard_map/all_to_all | solution.py:500
  42.8 0.0 copy-done.1
  42.8 0.0 copy-done
  42.8 10.9 %prefill.1 = bf16[512,1024]{1,0:T(8,128)(2,1)} custom-call(s32[64]{0:T(128)S(1)} %get-tuple-element.35.prefix_held, bf16[8,2,16,256]{3,2,1,0:T(8,128)(2,1)S(1)} %get-tuple-element.36.rest_0_, bf16[8,2,16,256]{3,2,1,0:T(8,128)(2,1)S(1)} %collective-permute-done.4.rest_1_, bf16[512,1024]{1,0:T(8,128)(2,1)S(1)} %bitcast.6, bf16[512,256]{1,0:T(8,128)(2,1)S(1)} %bitcast.7), custom_call_target="tpu_custom_call" | custom-call | flops 1610612736 | bytes 3000000 | tf_op jit(solution)/shard_map/prefill/pallas_call | solution.py:506
  53.7 3.6 %all-to-all-done.1.back = bf16[16,128,128]{2,1,0:T(8,128)(2,1)S(1)} async-done(((bf16[16,128,128]{2,1,0:T(8,128)(2,1)}), bf16[16,128,128]{2,1,0:T(8,128)(2,1)S(1)}, u32[]{:S(2)}, u32[]{:S(2)}) %all-to-all-start.1) | async-done | bytes 524320 | tf_op jit(solution)/shard_map/all_to_all | solution.py:500
  57.2 1.8 %unpack.1 = bf16[16,8192]{1,0:T(8,128)(2,1)} custom-call(s32[256]{0:T(256)} %bitcast.12, bf16[16,128,128]{2,1,0:T(8,128)(2,1)S(1)} %all-to-all-done.1.back), custom_call_target="tpu_custom_call" | custom-call | tf_op jit(solution)/shard_map/unpack/pallas_call | solution.py:531
Async XLA Ops:
  0.6 42.2 %copy-start.1 = (bf16[1,512,256]{2,1,0:T(8,128)(2,1)S(1)}, bf16[1,512,256]{2,1,0:T(8,128)(2,1)}, u32[]{:S(2)}) copy-start(bf16[1,512,256]{2,1,0:T(8,128)(2,1)} %param.14) | copy-start | bytes 786436
  0.6 42.2 %copy-start = (bf16[1,512,1024]{2,1,0:T(8,128)(2,1)S(1)}, bf16[1,512,1024]{2,1,0:T(8,128)(2,1)}, u32[]{:S(2)}) copy-start(bf16[1,512,1024]{2,1,0:T(8,128)(2,1)} %param.13) | copy-start | bytes 3145732
  3.0 26.3 %all-to-all-start = ((bf16[16,160,128]{2,1,0:T(8,128)(2,1)}), bf16[16,160,128]{2,1,0:T(8,128)(2,1)S(1)}, u32[]{:S(2)}, u32[]{:S(2)}) async-start(bf16[16,160,128]{2,1,0:T(8,128)(2,1)} %bitcast.9), calls=%async_computation | async-start | bytes 1310720 | tf_op jit(solution)/shard_map/all_to_all | solution.py:412
  12.7 2.2 %collective-permute-start = (bf16[2,2,2,16,256]{4,3,2,1,0:T(8,128)(2,1)S(1)}, bf16[2,2,2,16,256]{4,3,2,1,0:T(8,128)(2,1)S(1)}, u32[]{:S(2)}, u32[]{:S(2)}) collective-permute-start(bf16[2,2,2,16,256]{4,3,2,1,0:T(8,128)(2,1)S(1)} %get-tuple-element.24), channel_id=1, source_target_pairs={{0,1},{1,0},{2,3},{3,2},{4,5},{5,4},{6,7},{7,6},{8,9},{9,8},{10,11... | collective-permute-start | bytes 196616 | tf_op jit(solution)/shard_map/ppermute | solution.py:428
  13.2 6.4 %collective-permute-start.1 = (bf16[2,2,2,16,256]{4,3,2,1,0:T(8,128)(2,1)S(1)}, bf16[2,2,2,16,256]{4,3,2,1,0:T(8,128)(2,1)S(1)}, u32[]{:S(2)}, u32[]{:S(2)}) collective-permute-start(bf16[2,2,2,16,256]{4,3,2,1,0:T(8,128)(2,1)S(1)} %get-tuple-element.25), channel_id=1, source_target_pairs={{0,2},{1,3},{2,0},{3,1},{4,6},{5,7},{6,4},{7,5},{8,10},{9,11},{10,... | collective-permute-start | bytes 196616 | tf_op jit(solution)/shard_map/ppermute | solution.py:428
  14.8 6.5 %collective-permute-start.2 = (bf16[2,2,2,16,256]{4,3,2,1,0:T(8,128)(2,1)S(1)}, bf16[2,2,2,16,256]{4,3,2,1,0:T(8,128)(2,1)S(1)}, u32[]{:S(2)}, u32[]{:S(2)}) collective-permute-start(bf16[2,2,2,16,256]{4,3,2,1,0:T(8,128)(2,1)S(1)} %get-tuple-element.26), channel_id=1, source_target_pairs={{0,3},{1,2},{2,1},{3,0},{4,7},{5,6},{6,5},{7,4},{8,11},{9,10},{10,... | collective-permute-start | bytes 196616 | tf_op jit(solution)/shard_map/ppermute | solution.py:428
  21.5 7.3 %collective-permute-start.3 = (bf16[4,2,2,16,256]{4,3,2,1,0:T(8,128)(2,1)S(1)}, bf16[4,2,2,16,256]{4,3,2,1,0:T(8,128)(2,1)S(1)}, u32[]{:S(2)}, u32[]{:S(2)}) collective-permute-start(bf16[4,2,2,16,256]{4,3,2,1,0:T(8,128)(2,1)S(1)} %forward.1), channel_id=1, source_target_pairs={{0,4},{1,5},{2,6},{3,7},{4,0},{5,1},{6,2},{7,3},{8,12},{9,13},{10,... | collective-permute-start | bytes 393224 | tf_op jit(solution)/shard_map/ppermute | solution.py:441
  29.3 8.8 %collective-permute-start.4 = (bf16[8,2,16,256]{3,2,1,0:T(8,128)(2,1)S(1)}, bf16[8,2,16,256]{3,2,1,0:T(8,128)(2,1)S(1)}, u32[]{:S(2)}, u32[]{:S(2)}) collective-permute-start(bf16[8,2,16,256]{3,2,1,0:T(8,128)(2,1)S(1)} %get-tuple-element.33), channel_id=1, source_target_pairs={{0,8},{1,9},{2,10},{3,11},{4,12},{5,13},{6,14},{7,15},{8,0},{9,1},... | collective-permute-start | bytes 393224 | tf_op jit(solution)/shard_map/ppermute | solution.py:475
  38.1 19.1 %all-to-all-start.1 = ((bf16[16,128,128]{2,1,0:T(8,128)(2,1)}), bf16[16,128,128]{2,1,0:T(8,128)(2,1)S(1)}, u32[]{:S(2)}, u32[]{:S(2)}) async-start(bf16[16,128,128]{2,1,0:T(8,128)(2,1)} %decode.1), calls=%async_computation.1 | async-start | bytes 1048576 | tf_op jit(solution)/shard_map/all_to_all | solution.py:500

commit v4 on v1

--- a/solution.py
+++ b/solution.py
@@ -10,6 +10,7 @@
 PGRP = 8
 DGRP = 4
 PCAP = 2
+PLANE = 4
 LANES = 128
 MASKED = -1e30
 LOG2E = 1.4426950408889634
@@ -25,6 +26,10 @@
 
 def smem_spec():
     return pl.BlockSpec(memory_space=pltpu.SMEM)
+
+
+def in_hbm(x):
+    return pltpu.with_memory_space_constraint(x, pltpu.HBM)
 
 
 def vmem_spec():
@@ -84,7 +89,7 @@
 
 
 def blocks_kernel(table, count, pool, *rest):
-    outs, sems = rest[:PGRP], rest[PGRP]
+    outs, sems = rest[:PLANE], rest[PLANE]
     blocks_here = pool.shape[0]
     group_count, most_blocks = table.shape
     device = lax.axis_index("pool")
@@ -107,29 +112,38 @@
             for copy in flying.pop(0):
                 copy.wait()
         copies = []
-        for t in range(PGRP):
-            for k in range(PCAP):
-                copy = pltpu.make_async_copy(
-                    pool.at[chosen[k], (device % PGRP) ^ t],
-                    outs[t].at[g, k],
-                    sems.at[((g % 2) * PGRP + t) * PCAP + k],
-                )
-                copy.start()
-                copies.append(copy)
+        for half in range(PGRP // PLANE):
+            for t in range(PLANE):
+                for k in range(PCAP):
+                    copy = pltpu.make_async_copy(
+                        pool.at[chosen[k], half * PLANE + ((device % PLANE) ^ t)],
+                        outs[t].at[half, g, k],
+                        sems.at[((g % 2) * PGRP + half * PLANE + t) * PCAP + k],
+                    )
+                    copy.start()
+                    copies.append(copy)
         flying.append(copies)
     for copies in flying:
         for copy in copies:
             copy.wait()
 
 
-def regroup_kernel(group_count, *rest):
-    held, outs, sems = rest[:PGRP], rest[PGRP : PGRP + group_count], rest[-1]
-    mine = lax.axis_index("pool") // PGRP
+def partner(plane, step, planes):
+    return plane ^ step if planes & (planes - 1) == 0 else (plane + step) % planes
+
+
+def regroup_kernel(planes, *rest):
+    held, outs, sems = rest[:PLANE], rest[PLANE:-1], rest[-1]
+    mine = lax.axis_index("pool") // PLANE
+    per_group = PGRP // PLANE
     copies = []
-    for x in range(group_count):
-        for t in range(PGRP):
+    for step in range(planes):
+        there = partner(mine, step, planes)
+        for t in range(PLANE):
             copy = pltpu.make_async_copy(
-                held[t].at[(mine + x) % group_count], outs[x].at[t], sems.at[x * PGRP + t]
+                held[t].at[there % per_group, there // per_group],
+                outs[step].at[t],
+                sems.at[step * PLANE + t],
             )
             copy.start()
             copies.append(copy)
@@ -275,11 +289,11 @@
     lax.fori_loop(0, (live + width - 1) // width, several, 0)
 
 
-def prefill_kernel(group_count, tile, prefix_held, *rest):
-    sources = rest[:group_count]
-    q, new_kv, out, keys, values, bias = rest[group_count:]
+def prefill_kernel(planes, tile, prefix_held, *rest):
+    sources = rest[:planes]
+    q, new_kv, out, keys, values, bias = rest[planes:]
     blk = sources[0].shape[2]
-    prefix = group_count * PGRP * PCAP * blk
+    prefix = planes * PLANE * PCAP * blk
     token_count = new_kv.shape[0]
     scale = LANES ** (-0.5) * LOG2E
     device = lax.axis_index("pool")
@@ -288,13 +302,14 @@
     def _():
         lane_block = lax.broadcasted_iota(jnp.int32, (8, prefix), 1) // blk
         hide = jnp.zeros((8, prefix), jnp.float32)
-        for x in range(group_count):
-            sender = (device // PGRP - x + group_count) % group_count
-            for t in range(PGRP):
-                owner = sender * PGRP + ((device % PGRP) ^ t)
+        for step in range(planes):
+            sender = device // PLANE
+            sender = sender ^ step if planes & (planes - 1) == 0 else (sender + planes - step) % planes
+            for t in range(PLANE):
+                owner = sender * PLANE + ((device % PLANE) ^ t)
                 for k in range(PCAP):
-                    ordinal = (x * PGRP + t) * PCAP + k
-                    block = sources[x][t, k]
+                    ordinal = (step * PLANE + t) * PCAP + k
+                    block = sources[step][t, k]
                     keys[ordinal * blk : (ordinal + 1) * blk, :] = block[:, :LANES]
                     values[ordinal * blk : (ordinal + 1) * blk, :] = block[:, LANES:]
                     gone = jnp.where(prefix_held[owner] > k, 0.0, MASKED)
@@ -373,7 +388,6 @@
     groups = decode_group.reshape(-1)
     prefill_groups = prefix_table.shape[0]
     big = pltpu.CompilerParams(vmem_limit_bytes=60 * 2**20)
-    part = pltpu.CompilerParams(vmem_limit_bytes=52 * 2**20)
     small = pltpu.CompilerParams(vmem_limit_bytes=8 * 2**20)
 
     sending = pl.pallas_call(
@@ -389,47 +403,28 @@
         ],
         compiler_params=big,
         name="pack",
-    )(groups, decode_q, decode_new)
+    )(in_hbm(groups), in_hbm(decode_q), in_hbm(decode_new))
     sending = sending.reshape(devices, message_rows, LANES)
 
     received = lax.all_to_all(sending, "pool", split_axis=0, concat_axis=0, tiled=True)
 
-    share = jax.ShapeDtypeStruct((prefill_groups, PCAP, blk, 2 * LANES), jnp.bfloat16)
+    share = jax.ShapeDtypeStruct(
+        (PGRP // PLANE, prefill_groups, PCAP, blk, 2 * LANES), jnp.bfloat16
+    )
     shares = pl.pallas_call(
         blocks_kernel,
-        out_shape=(share,) * PGRP,
+        out_shape=(share,) * PLANE,
         in_specs=[smem_spec(), smem_spec(), any_spec()],
-        out_specs=(any_spec(),) * PGRP,
+        out_specs=(any_spec(),) * PLANE,
         scratch_shapes=[pltpu.SemaphoreType.DMA((2 * PGRP * PCAP,))],
         compiler_params=small,
         cost_estimate=pl.CostEstimate(flops=100000, bytes_accessed=1000000, transcendentals=0),
         name="blocks",
-    )(prefix_table, prefix_count, pool_kv)
+    )(in_hbm(prefix_table), in_hbm(prefix_count), in_hbm(pool_kv))
     shares = [shares[0]] + [
         lax.ppermute(shares[t], "pool", [(i, i ^ t) for i in range(devices)])
-        for t in range(1, PGRP)
+        for t in range(1, PLANE)
     ]
-    bundle = jax.ShapeDtypeStruct((PGRP, PCAP, blk, 2 * LANES), jnp.bfloat16)
-    bundles = pl.pallas_call(
-        functools.partial(regroup_kernel, prefill_groups),
-        out_shape=(bundle,) * prefill_groups,
-        in_specs=[any_spec()] * PGRP,
-        out_specs=(any_spec(),) * prefill_groups,
-        scratch_shapes=[pltpu.SemaphoreType.DMA((prefill_groups * PGRP,))],
-        compiler_params=small,
-        cost_estimate=pl.CostEstimate(flops=100000, bytes_accessed=1000000, transcendentals=0),
-        name="regroup",
-    )(*shares)
-    received, *bundles = lax.optimization_barrier((received, *bundles))
-    bundles = [bundles[0]] + [
-        lax.ppermute(
-            bundles[x],
-            "pool",
-            [(i, (i + x * PGRP) % devices) for i in range(devices)],
-        )
-        for x in range(1, prefill_groups)
-    ]
-
     chunk = min(cap, 4)
     width = 8
     block_count = devices * cap // chunk
@@ -445,7 +440,31 @@
         compiler_params=small,
         cost_estimate=pl.CostEstimate(flops=1000000, bytes_accessed=4000000, transcendentals=0),
         name="plan",
-    )(prefix_table, prefix_count, groups, cached_len)
+    )(in_hbm(prefix_table), in_hbm(prefix_count), in_hbm(groups), in_hbm(cached_len))
+
+    *shares, slot_len, listed = lax.optimization_barrier((*shares, slot_len, listed))
+    planes = devices // PLANE
+    bundle = jax.ShapeDtypeStruct((PLANE, PCAP, blk, 2 * LANES), jnp.bfloat16)
+    bundles = pl.pallas_call(
+        functools.partial(regroup_kernel, planes),
+        out_shape=(bundle,) * planes,
+        in_specs=[any_spec()] * PLANE,
+        out_specs=(any_spec(),) * planes,
+        scratch_shapes=[pltpu.SemaphoreType.DMA((planes * PLANE,))],
+        compiler_params=small,
+        cost_estimate=pl.CostEstimate(flops=100000, bytes_accessed=1000000, transcendentals=0),
+        name="regroup",
+    )(*shares)
+
+    def along_line(step):
+        pairs = [
+            (i, partner(i // PLANE, step, planes) * PLANE + i % PLANE) for i in range(devices)
+        ]
+        return lax.ppermute(bundles[step], "pool", pairs)
+
+    lines = [bundles[0], along_line(1)]
+
+    lines += [along_line(step) for step in range(2, planes)]
 
     answers = pl.pallas_call(
         functools.partial(decode_kernel, layout, chunk, width),
@@ -456,14 +475,14 @@
             pltpu.VMEM((block_count * chunk,) + decode_cache.shape[2:], jnp.bfloat16),
             pltpu.SemaphoreType.DMA((block_count,)),
         ],
-        compiler_params=part,
+        compiler_params=pltpu.CompilerParams(vmem_limit_bytes=20 * 2**20),
         cost_estimate=pl.CostEstimate(
             flops=500000000, bytes_accessed=8000000, transcendentals=1000000
         ),
         name="decode",
-    )(listed, slot_len, received, decode_cache[0])
-
-    answers, *bundles = lax.optimization_barrier((answers, *bundles))
+    )(listed, slot_len, received, in_hbm(decode_cache[0]))
+
+    answers, *lines = lax.optimization_barrier((answers, *lines))
     back = lax.all_to_all(answers, "pool", split_axis=0, concat_axis=0, tiled=True)
 
     token_count, fill_width = prefill_q.shape[1:]
@@ -471,11 +490,11 @@
     head_count = fill_width // LANES
     prefix_held, _ = lax.optimization_barrier((prefix_held, answers))
     prefill_out = pl.pallas_call(
-        functools.partial(prefill_kernel, prefill_groups, min(256, token_count)),
+        functools.partial(prefill_kernel, planes, min(256, token_count)),
         grid=(head_count,),
         out_shape=jax.ShapeDtypeStruct((token_count, fill_width), jnp.bfloat16),
         in_specs=[smem_spec()]
-        + [pl.BlockSpec(bundle.shape, lambda u: (0, 0, 0, 0))] * prefill_groups
+        + [pl.BlockSpec(bundle.shape, lambda u: (0, 0, 0, 0))] * planes
         + [
             pl.BlockSpec((token_count, LANES), lambda u: (0, u)),
             pl.BlockSpec(prefill_new_kv.shape[1:], lambda u: (0, 0)),
@@ -493,7 +512,7 @@
             transcendentals=token_count * head_count * (prefix + token_count // 2),
         ),
         name="prefill",
-    )(prefix_held, *bundles, prefill_q[0], prefill_new_kv[0])
+    )(prefix_held, *lines, prefill_q[0], prefill_new_kv[0])
 
     decode_out = pl.pallas_call(
         functools.partial(unpack_kernel, cap, head_rows),
@@ -506,7 +525,7 @@
         ],
         compiler_params=small,
         name="unpack",
-    )(groups, back)
+    )(in_hbm(groups), back)
     return (prefill_out[None], decode_out)
 
 

time: 64.1 us -> 57.9 us (0.903); the launches traced: 63.2 us -> 57.6 us
  local copies, waits for them, and re-layouts: 4.98 us -> 0.01 us
  Pallas kernels: 26.6 us -> 28.9 us
  waiting for transfers between devices: 9.48 us -> 7.89 us
  starting transfers between devices: 21.3 us -> 20 us
    ppermute x7 -> x3, starting transfers between devices: 7.35 us -> 2.16 us  [shards(): lax.ppermute(shares[t], 'pool', [(i, i ^ t) for i in range(devices)])]
    unnamed x20 -> x4, local copies, waits for them, and re-layouts: 4.98 us -> 0.01 us
    ppermute x7 -> x3, waiting for transfers between devices: 5.87 us -> 3.27 us  [shards(): lax.ppermute(shares[t], 'pool', [(i, i ^ t) for i in range(devices)])]
    all_to_all x1, starting transfers between devices: 3.74 us -> 6.06 us  [shards(): lax.all_to_all(answers, 'pool', split_axis=0, concat_axis=0, tiled=True)]
    ppermute x1 -> x3, starting transfers between devices: 2.83 us -> 4.45 us  [along_line(): return lax.ppermute(bundles[step], 'pool', pairs)]
    pallas_call x1, Pallas kernels: 6.79 us -> 8 us  [shards(): pl.pallas_call(functools.partial(decode_kernel, layout, chunk, width), ou...]
    all_to_all x1, waiting for transfers between devices: 0.01 us -> 1.03 us  [shards(): lax.all_to_all(sending, 'pool', split_axis=0, concat_axis=0, tiled=True)]
  transfers between devices with their start and end apart: 10 -> 8, of which waited for: 5 -> 4; matrix products, arithmetic and copies ran while one was open for 0% -> 0% of each run, Pallas kernels for 36% -> 43%
where the time goes in v4:
time: 57.9 us; the launch traced here: 57.6 us
  Pallas kernels  28.9 us (50%)
  starting transfers between devices  20 us (35%)
  waiting for transfers between devices  7.89 us (14%)
  between operations  0.76 us (1%)
    pallas_call x1, Pallas kernels, shards(): pl.pallas_call(functools.partial(prefill_kernel, planes, min(256, token_c...  10.9 us
    pallas_call x1, Pallas kernels, shards(): pl.pallas_call(functools.partial(decode_kernel, layout, chunk, width), ou...  8 us
    all_to_all x1, starting transfers between devices, shards(): lax.all_to_all(sending, 'pool', split_axis=0, concat_axis=0, tiled=True)  7.37 us
    all_to_all x1, starting transfers between devices, shards(): lax.all_to_all(answers, 'pool', split_axis=0, concat_axis=0, tiled=True)  6.06 us
    ppermute x3, starting transfers between devices, along_line(): return lax.ppermute(bundles[step], 'pool', pairs)  4.45 us
    all_to_all x1, waiting for transfers between devices, shards(): lax.all_to_all(answers, 'pool', split_axis=0, concat_axis=0, tiled=True)  3.57 us
    ppermute x3, waiting for transfers between devices, shards(): lax.ppermute(shares[t], 'pool', [(i, i ^ t) for i in range(devices)])  3.27 us
    pallas_call x1, Pallas kernels, shards(): pl.pallas_call(functools.partial(plan_kernel, cap, chunk, devices), out_s...  3.15 us
  transfers between devices with their start and end apart: 8, of which 4 were waited for; matrix products, arithmetic and copies ran while one was open for 0% of the time, Pallas kernels for 43%

profile of v4, /device:TPU:0, one launch (start us, length us, event | category | flops | bytes accessed | tf_op | source)
XLA Modules:
  0.0 57.6 jit_solution(10473379401646174556)
XLA Ops:
  0.6 0.0 copy-start.1
  0.6 0.0 copy-start
  0.7 2.4 %pack.1 = bf16[4,4,160,128]{3,2,1,0:T(8,128)(2,1)} custom-call(s32[256]{0:T(256)} %bitcast.10, bf16[16,8192]{1,0:T(8,128)(2,1)} %q.1, bf16[16,2048]{1,0:T(8,128)(2,1)} %kv.1), custom_call_target="tpu_custom_call" | custom-call | tf_op jit(solution)/shard_map/pack/pallas_call | solution.py:393
  3.0 7.4 %all-to-all-start = ((bf16[16,160,128]{2,1,0:T(8,128)(2,1)}), bf16[16,160,128]{2,1,0:T(8,128)(2,1)S(1)}, u32[]{:S(2)}, u32[]{:S(2)}) async-start(bf16[16,160,128]{2,1,0:T(8,128)(2,1)} %bitcast.9), calls=%async_computation | async-start | bytes 1310720 | tf_op jit(solution)/shard_map/all_to_all | solution.py:409
  10.4 2.3 %blocks.1 = (bf16[2,2,2,16,256]{4,3,2,1,0:T(8,128)(2,1)S(1)}, bf16[2,2,2,16,256]{4,3,2,1,0:T(8,128)(2,1)S(1)}, bf16[2,2,2,16,256]{4,3,2,1,0:T(8,128)(2,1)S(1)}, bf16[2,2,2,16,256]{4,3,2,1,0:T(8,128)(2,1)S(1)}) custom-call(s32[2,32]{1,0:T(2,128)} %table.3, s32[2]{0:T(128)} %count.3, bf16[4,8,16,256]{3,2,1,0:T(8,128)(2,1)} %pool.1), custom_call_target="tpu_custom_call" | custom-call | flops 100000 | bytes 1000000 | tf_op jit(solution)/shard_map/blocks/pallas_call | solution.py:414
  12.7 0.5 collective-permute-start
  13.2 1.7 %collective-permute-start.1 = (bf16[2,2,2,16,256]{4,3,2,1,0:T(8,128)(2,1)S(1)}, bf16[2,2,2,16,256]{4,3,2,1,0:T(8,128)(2,1)S(1)}, u32[]{:S(2)}, u32[]{:S(2)}) collective-permute-start(bf16[2,2,2,16,256]{4,3,2,1,0:T(8,128)(2,1)S(1)} %get-tuple-element.28), channel_id=1, source_target_pairs={{0,2},{1,3},{2,0},{3,1},{4,6},{5,7},{6,4},{7,5},{8,10},{9,11},{10,... | collective-permute-start | bytes 196616 | tf_op jit(solution)/shard_map/ppermute | solution.py:425
  14.8 0.0 collective-permute-start.2
  14.9 3.2 %plan.1 = (s32[128]{0:T(128)S(1)}, s32[34]{0:T(128)S(1)}, s32[64]{0:T(128)S(1)}) custom-call(s32[2,32]{1,0:T(2,128)} %table.3, s32[2]{0:T(128)} %count.3, s32[256]{0:T(256)} %bitcast.11, s32[256]{0:T(256)} %lengths.1), custom_call_target="tpu_custom_call" | custom-call | flops 1000000 | bytes 4000000 | tf_op jit(solution)/shard_map/plan/pallas_call | solution.py:431
  18.0 0.0 collective-permute-done.rest_1_
  18.0 1.5 %collective-permute-done.1.rest_2_ = bf16[2,2,2,16,256]{4,3,2,1,0:T(8,128)(2,1)S(1)} collective-permute-done((bf16[2,2,2,16,256]{4,3,2,1,0:T(8,128)(2,1)S(1)}, bf16[2,2,2,16,256]{4,3,2,1,0:T(8,128)(2,1)S(1)}, u32[]{:S(2)}, u32[]{:S(2)}) %collective-permute-start.1) | collective-permute-done | bytes 65568 | tf_op jit(solution)/shard_map/ppermute | solution.py:425
  19.6 1.7 %collective-permute-done.2.rest_3_ = bf16[2,2,2,16,256]{4,3,2,1,0:T(8,128)(2,1)S(1)} collective-permute-done((bf16[2,2,2,16,256]{4,3,2,1,0:T(8,128)(2,1)S(1)}, bf16[2,2,2,16,256]{4,3,2,1,0:T(8,128)(2,1)S(1)}, u32[]{:S(2)}, u32[]{:S(2)}) %collective-permute-start.2) | collective-permute-done | bytes 65568 | tf_op jit(solution)/shard_map/ppermute | solution.py:425
  21.3 0.5 regroup.1
  21.8 1.3 %collective-permute-start.3 = (bf16[4,2,16,256]{3,2,1,0:T(8,128)(2,1)S(1)}, bf16[4,2,16,256]{3,2,1,0:T(8,128)(2,1)S(1)}, u32[]{:S(2)}, u32[]{:S(2)}) collective-permute-start(bf16[4,2,16,256]{3,2,1,0:T(8,128)(2,1)S(1)} %get-tuple-element.39), channel_id=1, source_target_pairs={{0,4},{1,5},{2,6},{3,7},{4,0},{5,1},{6,2},{7,3},{8,12},{9,13},{10,... | collective-permute-start | bytes 196616 | tf_op jit(solution)/shard_map/ppermute | solution.py:463
  23.1 2.7 %collective-permute-start.4 = (bf16[4,2,16,256]{3,2,1,0:T(8,128)(2,1)S(1)}, bf16[4,2,16,256]{3,2,1,0:T(8,128)(2,1)S(1)}, u32[]{:S(2)}, u32[]{:S(2)}) collective-permute-start(bf16[4,2,16,256]{3,2,1,0:T(8,128)(2,1)S(1)} %get-tuple-element.40), channel_id=1, source_target_pairs={{0,8},{1,9},{2,10},{3,11},{4,12},{5,13},{6,14},{7,15},{8,0},{9,1},... | collective-permute-start | bytes 196616 | tf_op jit(solution)/shard_map/ppermute | solution.py:463
  25.9 0.4 collective-permute-start.5
  26.3 1.0 %all-to-all-done.recv = bf16[16,160,128]{2,1,0:T(8,128)(2,1)S(1)} async-done(((bf16[16,160,128]{2,1,0:T(8,128)(2,1)}), bf16[16,160,128]{2,1,0:T(8,128)(2,1)S(1)}, u32[]{:S(2)}, u32[]{:S(2)}) %all-to-all-start) | async-done | bytes 655392 | tf_op jit(solution)/shard_map/all_to_all | solution.py:409
  27.3 8.0 %decode.1 = bf16[16,128,128]{2,1,0:T(8,128)(2,1)} custom-call(s32[34]{0:T(128)S(1)} %get-tuple-element.32.listed, s32[128]{0:T(128)S(1)} %get-tuple-element.33.slot_len, bf16[16,160,128]{2,1,0:T(8,128)(2,1)S(1)} %all-to-all-done.recv, bf16[128,2,64,256]{3,2,1,0:T(8,128)(2,1)} %bitcast.8), custom_call_target="tpu_custom_call" | custom-call | flops 500000000 | bytes 8000000 | tf_op jit(solution)/shard_map/decode/pallas_call | solution.py:469
  35.3 0.0 collective-permute-done.3.rest_1_
  35.3 0.0 collective-permute-done.4.rest_2_
  35.3 0.0 collective-permute-done.5.rest_3_
  35.3 6.1 %all-to-all-start.1 = ((bf16[16,128,128]{2,1,0:T(8,128)(2,1)}), bf16[16,128,128]{2,1,0:T(8,128)(2,1)S(1)}, u32[]{:S(2)}, u32[]{:S(2)}) async-start(bf16[16,128,128]{2,1,0:T(8,128)(2,1)} %decode.1), calls=%async_computation.1 | async-start | bytes 1048576 | tf_op jit(solution)/shard_map/all_to_all | solution.py:486
  41.4 0.0 copy-done.1
  41.4 0.0 copy-done
  41.4 10.9 %prefill.1 = bf16[512,1024]{1,0:T(8,128)(2,1)} custom-call(s32[64]{0:T(128)S(1)} %get-tuple-element.43.prefix_held, bf16[4,2,16,256]{3,2,1,0:T(8,128)(2,1)S(1)} %get-tuple-element.44.rest_0_, bf16[4,2,16,256]{3,2,1,0:T(8,128)(2,1)S(1)} %collective-permute-done.3.rest_1_, bf16[4,2,16,256]{3,2,1,0:T(8,128)(2,1)S(1)} %collective-permute-done.4.rest_2_, ...), custom_call_target="tpu_custom_call" | custom-call | flops 1610612736 | bytes 3000000 | tf_op jit(solution)/shard_map/prefill/pallas_call | solution.py:492
  52.3 3.6 %all-to-all-done.1.back = bf16[16,128,128]{2,1,0:T(8,128)(2,1)S(1)} async-done(((bf16[16,128,128]{2,1,0:T(8,128)(2,1)}), bf16[16,128,128]{2,1,0:T(8,128)(2,1)S(1)}, u32[]{:S(2)}, u32[]{:S(2)}) %all-to-all-start.1) | async-done | bytes 524320 | tf_op jit(solution)/shard_map/all_to_all | solution.py:486
  55.9 1.8 %unpack.1 = bf16[16,8192]{1,0:T(8,128)(2,1)} custom-call(s32[256]{0:T(256)} %bitcast.12, bf16[16,128,128]{2,1,0:T(8,128)(2,1)S(1)} %all-to-all-done.1.back), custom_call_target="tpu_custom_call" | custom-call | tf_op jit(solution)/shard_map/unpack/pallas_call | solution.py:517
Async XLA Ops:
  0.6 40.8 %copy-start.1 = (bf16[1,512,256]{2,1,0:T(8,128)(2,1)S(1)}, bf16[1,512,256]{2,1,0:T(8,128)(2,1)}, u32[]{:S(2)}) copy-start(bf16[1,512,256]{2,1,0:T(8,128)(2,1)} %param.14) | copy-start | bytes 786436
  0.6 40.8 %copy-start = (bf16[1,512,1024]{2,1,0:T(8,128)(2,1)S(1)}, bf16[1,512,1024]{2,1,0:T(8,128)(2,1)}, u32[]{:S(2)}) copy-start(bf16[1,512,1024]{2,1,0:T(8,128)(2,1)} %param.13) | copy-start | bytes 3145732
  3.0 24.3 %all-to-all-start = ((bf16[16,160,128]{2,1,0:T(8,128)(2,1)}), bf16[16,160,128]{2,1,0:T(8,128)(2,1)S(1)}, u32[]{:S(2)}, u32[]{:S(2)}) async-start(bf16[16,160,128]{2,1,0:T(8,128)(2,1)} %bitcast.9), calls=%async_computation | async-start | bytes 1310720 | tf_op jit(solution)/shard_map/all_to_all | solution.py:409
  12.7 5.3 %collective-permute-start = (bf16[2,2,2,16,256]{4,3,2,1,0:T(8,128)(2,1)S(1)}, bf16[2,2,2,16,256]{4,3,2,1,0:T(8,128)(2,1)S(1)}, u32[]{:S(2)}, u32[]{:S(2)}) collective-permute-start(bf16[2,2,2,16,256]{4,3,2,1,0:T(8,128)(2,1)S(1)} %get-tuple-element.27), channel_id=1, source_target_pairs={{0,1},{1,0},{2,3},{3,2},{4,5},{5,4},{6,7},{7,6},{8,9},{9,8},{10,11... | collective-permute-start | bytes 196616 | tf_op jit(solution)/shard_map/ppermute | solution.py:425
  13.2 6.4 %collective-permute-start.1 = (bf16[2,2,2,16,256]{4,3,2,1,0:T(8,128)(2,1)S(1)}, bf16[2,2,2,16,256]{4,3,2,1,0:T(8,128)(2,1)S(1)}, u32[]{:S(2)}, u32[]{:S(2)}) collective-permute-start(bf16[2,2,2,16,256]{4,3,2,1,0:T(8,128)(2,1)S(1)} %get-tuple-element.28), channel_id=1, source_target_pairs={{0,2},{1,3},{2,0},{3,1},{4,6},{5,7},{6,4},{7,5},{8,10},{9,11},{10,... | collective-permute-start | bytes 196616 | tf_op jit(solution)/shard_map/ppermute | solution.py:425
  14.8 6.4 %collective-permute-start.2 = (bf16[2,2,2,16,256]{4,3,2,1,0:T(8,128)(2,1)S(1)}, bf16[2,2,2,16,256]{4,3,2,1,0:T(8,128)(2,1)S(1)}, u32[]{:S(2)}, u32[]{:S(2)}) collective-permute-start(bf16[2,2,2,16,256]{4,3,2,1,0:T(8,128)(2,1)S(1)} %get-tuple-element.29), channel_id=1, source_target_pairs={{0,3},{1,2},{2,1},{3,0},{4,7},{5,6},{6,5},{7,4},{8,11},{9,10},{10,... | collective-permute-start | bytes 196616 | tf_op jit(solution)/shard_map/ppermute | solution.py:425
  21.8 13.5 %collective-permute-start.3 = (bf16[4,2,16,256]{3,2,1,0:T(8,128)(2,1)S(1)}, bf16[4,2,16,256]{3,2,1,0:T(8,128)(2,1)S(1)}, u32[]{:S(2)}, u32[]{:S(2)}) collective-permute-start(bf16[4,2,16,256]{3,2,1,0:T(8,128)(2,1)S(1)} %get-tuple-element.39), channel_id=1, source_target_pairs={{0,4},{1,5},{2,6},{3,7},{4,0},{5,1},{6,2},{7,3},{8,12},{9,13},{10,... | collective-permute-start | bytes 196616 | tf_op jit(solution)/shard_map/ppermute | solution.py:463
  23.1 12.2 %collective-permute-start.4 = (bf16[4,2,16,256]{3,2,1,0:T(8,128)(2,1)S(1)}, bf16[4,2,16,256]{3,2,1,0:T(8,128)(2,1)S(1)}, u32[]{:S(2)}, u32[]{:S(2)}) collective-permute-start(bf16[4,2,16,256]{3,2,1,0:T(8,128)(2,1)S(1)} %get-tuple-element.40), channel_id=1, source_target_pairs={{0,8},{1,9},{2,10},{3,11},{4,12},{5,13},{6,14},{7,15},{8,0},{9,1},... | collective-permute-start | bytes 196616 | tf_op jit(solution)/shard_map/ppermute | solution.py:463
  25.9 9.5 %collective-permute-start.5 = (bf16[4,2,16,256]{3,2,1,0:T(8,128)(2,1)S(1)}, bf16[4,2,16,256]{3,2,1,0:T(8,128)(2,1)S(1)}, u32[]{:S(2)}, u32[]{:S(2)}) collective-permute-start(bf16[4,2,16,256]{3,2,1,0:T(8,128)(2,1)S(1)} %get-tuple-element.41), channel_id=1, source_target_pairs={{0,12},{1,13},{2,14},{3,15},{4,8},{5,9},{6,10},{7,11},{8,4},{9,5},... | collective-permute-start | bytes 196616 | tf_op jit(solution)/shard_map/ppermute | solution.py:463
  35.3 20.5 %all-to-all-start.1 = ((bf16[16,128,128]{2,1,0:T(8,128)(2,1)}), bf16[16,128,128]{2,1,0:T(8,128)(2,1)S(1)}, u32[]{:S(2)}, u32[]{:S(2)}) async-start(bf16[16,128,128]{2,1,0:T(8,128)(2,1)} %decode.1), calls=%async_computation.1 | async-start | bytes 1048576 | tf_op jit(solution)/shard_map/all_to_all | solution.py:486

commit v5 on v4

--- a/solution.py
+++ b/solution.py
@@ -464,6 +464,9 @@
 
     lines = [bundles[0], along_line(1)]
 
+    received, slot_len, listed, *bundles = lax.optimization_barrier(
+        (received, slot_len, listed, *bundles)
+    )
     lines += [along_line(step) for step in range(2, planes)]
 
     answers = pl.pallas_call(

time: 57.9 us -> 59 us (1.019); the launches traced: 57.6 us -> 59.4 us
  waiting for transfers between devices: 7.89 us -> 11.1 us
  Pallas kernels: 28.9 us -> 26.4 us
  starting transfers between devices: 20 us -> 21.1 us
    all_to_all x1, waiting for transfers between devices: 1.03 us -> 4.15 us  [shards(): lax.all_to_all(sending, 'pool', split_axis=0, concat_axis=0, tiled=True)]
    pallas_call x1, Pallas kernels: 8 us -> 5.56 us  [shards(): pl.pallas_call(functools.partial(decode_kernel, layout, chunk, width), ou...]
  transfers between devices with their start and end apart: 8 -> 8, of which waited for: 4 -> 4; matrix products, arithmetic and copies ran while one was open for 0% -> 0% of each run, Pallas kernels for 43% -> 37%
where the time goes in v5:
time: 59 us; the launch traced here: 59.4 us
  Pallas kernels  26.4 us (45%)
  starting transfers between devices  21.1 us (36%)
  waiting for transfers between devices  11.1 us (19%)
  between operations  0.76 us (1%)
    pallas_call x1, Pallas kernels, shards(): pl.pallas_call(functools.partial(prefill_kernel, planes, min(256, token_c...  10.9 us
    all_to_all x1, starting transfers between devices, shards(): lax.all_to_all(sending, 'pool', split_axis=0, concat_axis=0, tiled=True)  7.37 us
    all_to_all x1, starting transfers between devices, shards(): lax.all_to_all(answers, 'pool', split_axis=0, concat_axis=0, tiled=True)  6.59 us
    pallas_call x1, Pallas kernels, shards(): pl.pallas_call(functools.partial(decode_kernel, layout, chunk, width), ou...  5.56 us
    ppermute x3, starting transfers between devices, along_line(): return lax.ppermute(bundles[step], 'pool', pairs)  5.02 us
    all_to_all x1, waiting for transfers between devices, shards(): lax.all_to_all(sending, 'pool', split_axis=0, concat_axis=0, tiled=True)  4.15 us
    all_to_all x1, waiting for transfers between devices, shards(): lax.all_to_all(answers, 'pool', split_axis=0, concat_axis=0, tiled=True)  3.57 us
    ppermute x3, waiting for transfers between devices, shards(): lax.ppermute(shares[t], 'pool', [(i, i ^ t) for i in range(devices)])  3.41 us
  transfers between devices with their start and end apart: 8, of which 4 were waited for; matrix products, arithmetic and copies ran while one was open for 0% of the time, Pallas kernels for 37%

profile of v5, /device:TPU:0, one launch (start us, length us, event | category | flops | bytes accessed | tf_op | source)
XLA Modules:
  0.0 59.4 jit_solution(16693783676211916049)
XLA Ops:
  0.6 0.0 copy-start.1
  0.6 0.0 copy-start
  0.7 2.4 %pack.1 = bf16[4,4,160,128]{3,2,1,0:T(8,128)(2,1)} custom-call(s32[256]{0:T(256)} %bitcast.10, bf16[16,8192]{1,0:T(8,128)(2,1)} %q.1, bf16[16,2048]{1,0:T(8,128)(2,1)} %kv.1), custom_call_target="tpu_custom_call" | custom-call | tf_op jit(solution)/shard_map/pack/pallas_call | solution.py:393
  3.0 7.4 %all-to-all-start = ((bf16[16,160,128]{2,1,0:T(8,128)(2,1)}), bf16[16,160,128]{2,1,0:T(8,128)(2,1)S(1)}, u32[]{:S(2)}, u32[]{:S(2)}) async-start(bf16[16,160,128]{2,1,0:T(8,128)(2,1)} %bitcast.9), calls=%async_computation | async-start | bytes 1310720 | tf_op jit(solution)/shard_map/all_to_all | solution.py:409
  10.4 2.3 %blocks.1 = (bf16[2,2,2,16,256]{4,3,2,1,0:T(8,128)(2,1)S(1)}, bf16[2,2,2,16,256]{4,3,2,1,0:T(8,128)(2,1)S(1)}, bf16[2,2,2,16,256]{4,3,2,1,0:T(8,128)(2,1)S(1)}, bf16[2,2,2,16,256]{4,3,2,1,0:T(8,128)(2,1)S(1)}) custom-call(s32[2,32]{1,0:T(2,128)} %table.3, s32[2]{0:T(128)} %count.3, bf16[4,8,16,256]{3,2,1,0:T(8,128)(2,1)} %pool.1), custom_call_target="tpu_custom_call" | custom-call | flops 100000 | bytes 1000000 | tf_op jit(solution)/shard_map/blocks/pallas_call | solution.py:414
  12.7 0.5 collective-permute-start
  13.2 1.7 %collective-permute-start.1 = (bf16[2,2,2,16,256]{4,3,2,1,0:T(8,128)(2,1)S(1)}, bf16[2,2,2,16,256]{4,3,2,1,0:T(8,128)(2,1)S(1)}, u32[]{:S(2)}, u32[]{:S(2)}) collective-permute-start(bf16[2,2,2,16,256]{4,3,2,1,0:T(8,128)(2,1)S(1)} %get-tuple-element.33), channel_id=1, source_target_pairs={{0,2},{1,3},{2,0},{3,1},{4,6},{5,7},{6,4},{7,5},{8,10},{9,11},{10,... | collective-permute-start | bytes 196616 | tf_op jit(solution)/shard_map/ppermute | solution.py:425
  14.9 0.0 collective-permute-start.2
  14.9 3.0 %plan.1 = (s32[128]{0:T(128)S(1)}, s32[34]{0:T(128)S(1)}, s32[64]{0:T(128)S(1)}) custom-call(s32[2,32]{1,0:T(2,128)} %table.3, s32[2]{0:T(128)} %count.3, s32[256]{0:T(256)} %bitcast.11, s32[256]{0:T(256)} %lengths.1), custom_call_target="tpu_custom_call" | custom-call | flops 1000000 | bytes 4000000 | tf_op jit(solution)/shard_map/plan/pallas_call | solution.py:431
  17.9 0.0 collective-permute-done.rest_1_
  17.9 1.7 %collective-permute-done.1.rest_2_ = bf16[2,2,2,16,256]{4,3,2,1,0:T(8,128)(2,1)S(1)} collective-permute-done((bf16[2,2,2,16,256]{4,3,2,1,0:T(8,128)(2,1)S(1)}, bf16[2,2,2,16,256]{4,3,2,1,0:T(8,128)(2,1)S(1)}, u32[]{:S(2)}, u32[]{:S(2)}) %collective-permute-start.1) | collective-permute-done | bytes 65568 | tf_op jit(solution)/shard_map/ppermute | solution.py:425
  19.6 1.7 %collective-permute-done.2.rest_3_ = bf16[2,2,2,16,256]{4,3,2,1,0:T(8,128)(2,1)S(1)} collective-permute-done((bf16[2,2,2,16,256]{4,3,2,1,0:T(8,128)(2,1)S(1)}, bf16[2,2,2,16,256]{4,3,2,1,0:T(8,128)(2,1)S(1)}, u32[]{:S(2)}, u32[]{:S(2)}) %collective-permute-start.2) | collective-permute-done | bytes 65568 | tf_op jit(solution)/shard_map/ppermute | solution.py:425
  21.3 0.5 regroup.1
  21.8 1.3 %collective-permute-start.3 = (bf16[4,2,16,256]{3,2,1,0:T(8,128)(2,1)S(1)}, bf16[4,2,16,256]{3,2,1,0:T(8,128)(2,1)S(1)}, u32[]{:S(2)}, u32[]{:S(2)}) collective-permute-start(bf16[4,2,16,256]{3,2,1,0:T(8,128)(2,1)S(1)} %get-tuple-element.44), channel_id=1, source_target_pairs={{0,4},{1,5},{2,6},{3,7},{4,0},{5,1},{6,2},{7,3},{8,12},{9,13},{10,... | collective-permute-start | bytes 196616 | tf_op jit(solution)/shard_map/ppermute | solution.py:463
  23.1 4.2 %all-to-all-done.recv = bf16[16,160,128]{2,1,0:T(8,128)(2,1)S(1)} async-done(((bf16[16,160,128]{2,1,0:T(8,128)(2,1)}), bf16[16,160,128]{2,1,0:T(8,128)(2,1)S(1)}, u32[]{:S(2)}, u32[]{:S(2)}) %all-to-all-start) | async-done | bytes 655392 | tf_op jit(solution)/shard_map/all_to_all | solution.py:409
  27.3 2.6 %collective-permute-start.4 = (bf16[4,2,16,256]{3,2,1,0:T(8,128)(2,1)S(1)}, bf16[4,2,16,256]{3,2,1,0:T(8,128)(2,1)S(1)}, u32[]{:S(2)}, u32[]{:S(2)}) collective-permute-start(bf16[4,2,16,256]{3,2,1,0:T(8,128)(2,1)S(1)} %get-tuple-element.50), channel_id=1, source_target_pairs={{0,8},{1,9},{2,10},{3,11},{4,12},{5,13},{6,14},{7,15},{8,0},{9,1},... | collective-permute-start | bytes 196616 | tf_op jit(solution)/shard_map/ppermute | solution.py:463
  29.9 1.1 %collective-permute-start.5 = (bf16[4,2,16,256]{3,2,1,0:T(8,128)(2,1)S(1)}, bf16[4,2,16,256]{3,2,1,0:T(8,128)(2,1)S(1)}, u32[]{:S(2)}, u32[]{:S(2)}) collective-permute-start(bf16[4,2,16,256]{3,2,1,0:T(8,128)(2,1)S(1)} %get-tuple-element.51), channel_id=1, source_target_pairs={{0,12},{1,13},{2,14},{3,15},{4,8},{5,9},{6,10},{7,11},{8,4},{9,5},... | collective-permute-start | bytes 196616 | tf_op jit(solution)/shard_map/ppermute | solution.py:463
  31.0 5.6 %decode.1 = bf16[16,128,128]{2,1,0:T(8,128)(2,1)} custom-call(s32[34]{0:T(128)S(1)} %get-tuple-element.47.listed, s32[128]{0:T(128)S(1)} %get-tuple-element.48.slot_len, bf16[16,160,128]{2,1,0:T(8,128)(2,1)S(1)} %all-to-all-done.recv, bf16[128,2,64,256]{3,2,1,0:T(8,128)(2,1)} %bitcast.8), custom_call_target="tpu_custom_call" | custom-call | flops 500000000 | bytes 8000000 | tf_op jit(solution)/shard_map/decode/pallas_call | solution.py:472
  36.6 0.0 collective-permute-done.3.rest_1_
  36.6 0.0 collective-permute-done.4.rest_2_
  36.6 0.0 collective-permute-done.5.rest_3_
  36.6 6.6 %all-to-all-start.1 = ((bf16[16,128,128]{2,1,0:T(8,128)(2,1)}), bf16[16,128,128]{2,1,0:T(8,128)(2,1)S(1)}, u32[]{:S(2)}, u32[]{:S(2)}) async-start(bf16[16,128,128]{2,1,0:T(8,128)(2,1)} %decode.1), calls=%async_computation.1 | async-start | bytes 1048576 | tf_op jit(solution)/shard_map/all_to_all | solution.py:489
  43.2 0.0 copy-done.1
  43.2 0.0 copy-done
  43.2 10.9 %prefill.1 = bf16[512,1024]{1,0:T(8,128)(2,1)} custom-call(s32[64]{0:T(128)S(1)} %get-tuple-element.53.prefix_held, bf16[4,2,16,256]{3,2,1,0:T(8,128)(2,1)S(1)} %get-tuple-element.54.rest_0_, bf16[4,2,16,256]{3,2,1,0:T(8,128)(2,1)S(1)} %collective-permute-done.3.rest_1_, bf16[4,2,16,256]{3,2,1,0:T(8,128)(2,1)S(1)} %collective-permute-done.4.rest_2_, ...), custom_call_target="tpu_custom_call" | custom-call | flops 1610612736 | bytes 3000000 | tf_op jit(solution)/shard_map/prefill/pallas_call | solution.py:495
  54.1 3.6 %all-to-all-done.1.back = bf16[16,128,128]{2,1,0:T(8,128)(2,1)S(1)} async-done(((bf16[16,128,128]{2,1,0:T(8,128)(2,1)}), bf16[16,128,128]{2,1,0:T(8,128)(2,1)S(1)}, u32[]{:S(2)}, u32[]{:S(2)}) %all-to-all-start.1) | async-done | bytes 524320 | tf_op jit(solution)/shard_map/all_to_all | solution.py:489
  57.7 1.8 %unpack.1 = bf16[16,8192]{1,0:T(8,128)(2,1)} custom-call(s32[256]{0:T(256)} %bitcast.12, bf16[16,128,128]{2,1,0:T(8,128)(2,1)S(1)} %all-to-all-done.1.back), custom_call_target="tpu_custom_call" | custom-call | tf_op jit(solution)/shard_map/unpack/pallas_call | solution.py:520
Async XLA Ops:
  0.6 42.6 %copy-start.1 = (bf16[1,512,256]{2,1,0:T(8,128)(2,1)S(1)}, bf16[1,512,256]{2,1,0:T(8,128)(2,1)}, u32[]{:S(2)}) copy-start(bf16[1,512,256]{2,1,0:T(8,128)(2,1)} %param.14) | copy-start | bytes 786436
  0.6 42.6 %copy-start = (bf16[1,512,1024]{2,1,0:T(8,128)(2,1)S(1)}, bf16[1,512,1024]{2,1,0:T(8,128)(2,1)}, u32[]{:S(2)}) copy-start(bf16[1,512,1024]{2,1,0:T(8,128)(2,1)} %param.13) | copy-start | bytes 3145732
  3.0 24.3 %all-to-all-start = ((bf16[16,160,128]{2,1,0:T(8,128)(2,1)}), bf16[16,160,128]{2,1,0:T(8,128)(2,1)S(1)}, u32[]{:S(2)}, u32[]{:S(2)}) async-start(bf16[16,160,128]{2,1,0:T(8,128)(2,1)} %bitcast.9), calls=%async_computation | async-start | bytes 1310720 | tf_op jit(solution)/shard_map/all_to_all | solution.py:409
  12.7 5.2 %collective-permute-start = (bf16[2,2,2,16,256]{4,3,2,1,0:T(8,128)(2,1)S(1)}, bf16[2,2,2,16,256]{4,3,2,1,0:T(8,128)(2,1)S(1)}, u32[]{:S(2)}, u32[]{:S(2)}) collective-permute-start(bf16[2,2,2,16,256]{4,3,2,1,0:T(8,128)(2,1)S(1)} %get-tuple-element.32), channel_id=1, source_target_pairs={{0,1},{1,0},{2,3},{3,2},{4,5},{5,4},{6,7},{7,6},{8,9},{9,8},{10,11... | collective-permute-start | bytes 196616 | tf_op jit(solution)/shard_map/ppermute | solution.py:425
  13.2 6.4 %collective-permute-start.1 = (bf16[2,2,2,16,256]{4,3,2,1,0:T(8,128)(2,1)S(1)}, bf16[2,2,2,16,256]{4,3,2,1,0:T(8,128)(2,1)S(1)}, u32[]{:S(2)}, u32[]{:S(2)}) collective-permute-start(bf16[2,2,2,16,256]{4,3,2,1,0:T(8,128)(2,1)S(1)} %get-tuple-element.33), channel_id=1, source_target_pairs={{0,2},{1,3},{2,0},{3,1},{4,6},{5,7},{6,4},{7,5},{8,10},{9,11},{10,... | collective-permute-start | bytes 196616 | tf_op jit(solution)/shard_map/ppermute | solution.py:425
  14.9 6.4 %collective-permute-start.2 = (bf16[2,2,2,16,256]{4,3,2,1,0:T(8,128)(2,1)S(1)}, bf16[2,2,2,16,256]{4,3,2,1,0:T(8,128)(2,1)S(1)}, u32[]{:S(2)}, u32[]{:S(2)}) collective-permute-start(bf16[2,2,2,16,256]{4,3,2,1,0:T(8,128)(2,1)S(1)} %get-tuple-element.34), channel_id=1, source_target_pairs={{0,3},{1,2},{2,1},{3,0},{4,7},{5,6},{6,5},{7,4},{8,11},{9,10},{10,... | collective-permute-start | bytes 196616 | tf_op jit(solution)/shard_map/ppermute | solution.py:425
  21.8 14.7 %collective-permute-start.3 = (bf16[4,2,16,256]{3,2,1,0:T(8,128)(2,1)S(1)}, bf16[4,2,16,256]{3,2,1,0:T(8,128)(2,1)S(1)}, u32[]{:S(2)}, u32[]{:S(2)}) collective-permute-start(bf16[4,2,16,256]{3,2,1,0:T(8,128)(2,1)S(1)} %get-tuple-element.44), channel_id=1, source_target_pairs={{0,4},{1,5},{2,6},{3,7},{4,0},{5,1},{6,2},{7,3},{8,12},{9,13},{10,... | collective-permute-start | bytes 196616 | tf_op jit(solution)/shard_map/ppermute | solution.py:463
  27.3 9.3 %collective-permute-start.4 = (bf16[4,2,16,256]{3,2,1,0:T(8,128)(2,1)S(1)}, bf16[4,2,16,256]{3,2,1,0:T(8,128)(2,1)S(1)}, u32[]{:S(2)}, u32[]{:S(2)}) collective-permute-start(bf16[4,2,16,256]{3,2,1,0:T(8,128)(2,1)S(1)} %get-tuple-element.50), channel_id=1, source_target_pairs={{0,8},{1,9},{2,10},{3,11},{4,12},{5,13},{6,14},{7,15},{8,0},{9,1},... | collective-permute-start | bytes 196616 | tf_op jit(solution)/shard_map/ppermute | solution.py:463
  29.9 6.6 %collective-permute-start.5 = (bf16[4,2,16,256]{3,2,1,0:T(8,128)(2,1)S(1)}, bf16[4,2,16,256]{3,2,1,0:T(8,128)(2,1)S(1)}, u32[]{:S(2)}, u32[]{:S(2)}) collective-permute-start(bf16[4,2,16,256]{3,2,1,0:T(8,128)(2,1)S(1)} %get-tuple-element.51), channel_id=1, source_target_pairs={{0,12},{1,13},{2,14},{3,15},{4,8},{5,9},{6,10},{7,11},{8,4},{9,5},... | collective-permute-start | bytes 196616 | tf_op jit(solution)/shard_map/ppermute | solution.py:463
  36.6 21.1 %all-to-all-start.1 = ((bf16[16,128,128]{2,1,0:T(8,128)(2,1)}), bf16[16,128,128]{2,1,0:T(8,128)(2,1)S(1)}, u32[]{:S(2)}, u32[]{:S(2)}) async-start(bf16[16,128,128]{2,1,0:T(8,128)(2,1)} %decode.1), calls=%async_computation.1 | async-start | bytes 1048576 | tf_op jit(solution)/shard_map/all_to_all | solution.py:489

commit v6 on v5

--- a/solution.py
+++ b/solution.py
@@ -151,7 +151,15 @@
         copy.wait()
 
 
-def plan_kernel(cap, step, owners, table, count, groups, lengths, slot_len, listed, prefix_held):
+def fetch_block(cache, listed, i, chunk, held, place, sem):
+    return pltpu.make_async_copy(
+        cache.at[pl.ds(listed[1 + i] * chunk, chunk)], held.at[pl.ds(place * chunk, chunk)], sem
+    )
+
+
+def plan_kernel(
+    cap, step, owners, table, count, groups, lengths, cache, slot_len, listed, prefix_held, ahead, sems
+):
     device = lax.axis_index("pool")
     home_count = owners
     row_count = groups.shape[0] // home_count
@@ -190,10 +198,15 @@
             filled = filled + (here > b * chunk).astype(jnp.int32)
         return filled
 
-    listed[0] = lax.fori_loop(0, home_count, one_home, jnp.int32(0))
-
-
-def decode_kernel(layout, chunk, width, listed, slot_len, recv, cache, out, held, sems):
+    live = lax.fori_loop(0, home_count, one_home, jnp.int32(0))
+    listed[0] = live
+    for i in range(ahead.shape[0] // chunk):
+        pl.when(i < live)(fetch_block(cache, listed, i, chunk, ahead, i, sems.at[i]).start)
+    for i in range(ahead.shape[0] // chunk):
+        pl.when(i < live)(fetch_block(cache, listed, i, chunk, ahead, i, sems.at[i]).wait)
+
+
+def decode_kernel(layout, chunk, width, listed, slot_len, recv, ahead, cache, out, held, sems):
     cap, head_rows, own_rows, own_start = layout
     pair_count, positions = cache.shape[1], cache.shape[2]
     per_home = cap // chunk
@@ -203,19 +216,16 @@
     scale = LANES ** (-0.5) * LOG2E
     rows = chunk * head_rows
     slots = width * chunk
+    pair = 2 if chunk % 2 == 0 else 1
 
     def fetch(i):
-        return pltpu.make_async_copy(
-            cache.at[pl.ds(listed[1 + i] * chunk, chunk)],
-            held.at[pl.ds(i * chunk, chunk)],
-            sems.at[i],
-        )
+        return fetch_block(cache, listed, i, chunk, held, i - width, sems.at[i - width])
 
     def begin(i, carry):
         fetch(i).start()
         return carry
 
-    lax.fori_loop(0, live, begin, 0)
+    lax.fori_loop(width, live, begin, 0)
     row_pair = lax.broadcasted_iota(jnp.int32, (head_rows, key_count), 0) // query_heads
     key_axis = lax.broadcasted_iota(jnp.int32, (head_rows, key_count), 1)
     pos = jnp.where(key_axis // positions == row_pair, key_axis % positions, positions)
@@ -223,14 +233,8 @@
     own_row = lax.broadcasted_iota(jnp.int32, (rows, own_rows), 0)
     own_want = ((own_row % head_rows) // query_heads) * cap + own_row // head_rows
 
-    def several(t, carry):
+    def several(t, kv):
         ids = [jnp.minimum(t * width + w, live - 1) for w in range(width)]
-        for w in range(width):
-
-            @pl.when(t * width + w < live)
-            def _():
-                fetch(t * width + w).wait()
-
         blocks = [listed[1 + i] for i in ids]
         homes = [b // per_home for b in blocks]
         firsts = [(b % per_home) * chunk for b in blocks]
@@ -242,15 +246,18 @@
         own_values = jnp.stack(
             [recv[h, own_start + own_rows : own_start + 2 * own_rows, :] for h in homes]
         )
-        kv = held[pl.ds(t * slots, slots)]
         keys = kv[..., :LANES].reshape(slots, key_count, LANES)
         values = kv[..., LANES:].reshape(slots, key_count, LANES)
         scores = jnp.einsum(
             "jqd,jkd->jqk",
-            q.reshape(slots, head_rows, LANES),
-            keys,
+            q.reshape(slots // pair, pair * head_rows, LANES),
+            keys.reshape(slots // pair, pair * key_count, LANES),
             preferred_element_type=jnp.float32,
         )
+        if pair == 2:
+            scores = jnp.stack(
+                [scores[:, :head_rows, :key_count], scores[:, head_rows:, key_count:]], axis=1
+            ).reshape(slots, head_rows, key_count)
         kept = jnp.stack(
             [pos < slot_len[blocks[w] * chunk + j] for w in range(width) for j in range(chunk)]
         )
@@ -268,10 +275,17 @@
         weights = jnp.exp2((scores - top) * scale)
         own_weight = jnp.exp2((own_score - top) * scale)
         total = jnp.sum(weights, axis=2, keepdims=True) + own_weight
+        weights = weights.astype(jnp.bfloat16)
+        if pair == 2:
+            weights = weights.reshape(slots // 2, 2, head_rows, key_count)
+            nothing = jnp.zeros((slots // 2, head_rows, key_count), jnp.bfloat16)
+            upper = jnp.concatenate([weights[:, 0], nothing], axis=2)
+            lower = jnp.concatenate([nothing, weights[:, 1]], axis=2)
+            weights = jnp.concatenate([upper, lower], axis=1)
         mixed = jnp.einsum(
             "jqk,jkd->jqd",
-            weights.astype(jnp.bfloat16),
-            values,
+            weights,
+            values.reshape(slots // pair, pair * key_count, LANES),
             preferred_element_type=jnp.float32,
         )
         own_part = jnp.where(own_hit, own_weight.reshape(width, rows, 1), 0.0)
@@ -284,9 +298,16 @@
         mixed = mixed / total.reshape(width, rows, 1)
         for w in reversed(range(width)):
             out[homes[w], pl.ds(places[w], rows), :] = mixed[w].astype(out.dtype)
+
+    several(0, ahead[...])
+
+    def later(t, carry):
+        for w in range(width):
+            pl.when(t * width + w < live)(fetch(t * width + w).wait)
+        several(t, held[pl.ds((t - 1) * slots, slots)])
         return carry
 
-    lax.fori_loop(0, (live + width - 1) // width, several, 0)
+    lax.fori_loop(1, (live + width - 1) // width, later, 0)
 
 
 def prefill_kernel(planes, tile, prefix_held, *rest):
@@ -428,19 +449,21 @@
     chunk = min(cap, 4)
     width = 8
     block_count = devices * cap // chunk
-    slot_len, listed, prefix_held = pl.pallas_call(
+    slot_len, listed, prefix_held, ahead = pl.pallas_call(
         functools.partial(plan_kernel, cap, chunk, devices),
         out_shape=(
             jax.ShapeDtypeStruct((devices * cap,), jnp.int32),
             jax.ShapeDtypeStruct((block_count + 2,), jnp.int32),
             jax.ShapeDtypeStruct((devices * pool_kv.shape[0],), jnp.int32),
+            jax.ShapeDtypeStruct((width * chunk,) + decode_cache.shape[2:], jnp.bfloat16),
         ),
-        in_specs=[smem_spec()] * 4,
-        out_specs=(smem_spec(),) * 3,
+        in_specs=[smem_spec()] * 4 + [any_spec()],
+        out_specs=(smem_spec(),) * 3 + (vmem_spec(),),
+        scratch_shapes=[pltpu.SemaphoreType.DMA((width,))],
         compiler_params=small,
         cost_estimate=pl.CostEstimate(flops=1000000, bytes_accessed=4000000, transcendentals=0),
         name="plan",
-    )(in_hbm(prefix_table), in_hbm(prefix_count), in_hbm(groups), in_hbm(cached_len))
+    )(in_hbm(prefix_table), in_hbm(prefix_count), in_hbm(groups), in_hbm(cached_len), in_hbm(decode_cache[0]))
 
     *shares, slot_len, listed = lax.optimization_barrier((*shares, slot_len, listed))
     planes = devices // PLANE
@@ -472,18 +495,18 @@
     answers = pl.pallas_call(
         functools.partial(decode_kernel, layout, chunk, width),
         out_shape=jax.ShapeDtypeStruct((devices, cap * head_rows, LANES), jnp.bfloat16),
-        in_specs=[smem_spec(), smem_spec(), vmem_spec(), any_spec()],
+        in_specs=[smem_spec(), smem_spec(), vmem_spec(), vmem_spec(), any_spec()],
         out_specs=vmem_spec(),
         scratch_shapes=[
-            pltpu.VMEM((block_count * chunk,) + decode_cache.shape[2:], jnp.bfloat16),
-            pltpu.SemaphoreType.DMA((block_count,)),
+            pltpu.VMEM(((block_count - width) * chunk,) + decode_cache.shape[2:], jnp.bfloat16),
+            pltpu.SemaphoreType.DMA((block_count - width,)),
         ],
         compiler_params=pltpu.CompilerParams(vmem_limit_bytes=20 * 2**20),
         cost_estimate=pl.CostEstimate(
             flops=500000000, bytes_accessed=8000000, transcendentals=1000000
         ),
         name="decode",
-    )(listed, slot_len, received, in_hbm(decode_cache[0]))
+    )(listed, slot_len, received, ahead, in_hbm(decode_cache[0]))
 
     answers, *lines = lax.optimization_barrier((answers, *lines))
     back = lax.all_to_all(answers, "pool", split_axis=0, concat_axis=0, tiled=True)
@@ -515,7 +538,7 @@
             transcendentals=token_count * head_count * (prefix + token_count // 2),
         ),
         name="prefill",
-    )(prefix_held, *lines, prefill_q[0], prefill_new_kv[0])
+    )(prefix_held, *lines, in_hbm(prefill_q[0]), in_hbm(prefill_new_kv[0]))
 
     decode_out = pl.pallas_call(
         functools.partial(unpack_kernel, cap, head_rows),

time: 59 us -> 56.3 us (0.954); the launches traced: 59.4 us -> 55.8 us
  starting transfers between devices: 21.1 us -> 18.1 us
  waiting for transfers between devices: 11.1 us -> 10.3 us
    all_to_all x1, starting transfers between devices: 6.59 us -> 3.59 us  [shards(): lax.all_to_all(answers, 'pool', split_axis=0, concat_axis=0, tiled=True)]
    ppermute x3, waiting for transfers between devices: 3.41 us -> 1.68 us  [shards(): lax.ppermute(shares[t], 'pool', [(i, i ^ t) for i in range(devices)])]
    pallas_call x1, Pallas kernels: 3.02 us -> 4.74 us  [shards(): pl.pallas_call(functools.partial(plan_kernel, cap, chunk, devices), out_s...]
    pallas_call x1, Pallas kernels: 5.56 us -> 3.95 us  [shards(): pl.pallas_call(functools.partial(decode_kernel, layout, chunk, width), ou...]
    ppermute x3, waiting for transfers between devices: 0.01 us -> 1.15 us  [along_line(): return lax.ppermute(bundles[step], 'pool', pairs)]
  transfers between devices with their start and end apart: 8 -> 8, of which waited for: 4 -> 5; matrix products, arithmetic and copies ran while one was open for 0% -> 0% of each run, Pallas kernels for 37% -> 40%
where the time goes in v6:
time: 56.3 us; the launch traced here: 55.8 us
  Pallas kernels  26.6 us (47%)
  starting transfers between devices  18.1 us (32%)
  waiting for transfers between devices  10.3 us (18%)
  between operations  0.72 us (1%)
    pallas_call x1, Pallas kernels, shards(): pl.pallas_call(functools.partial(prefill_kernel, planes, min(256, token_c...  11.1 us
    all_to_all x1, starting transfers between devices, shards(): lax.all_to_all(sending, 'pool', split_axis=0, concat_axis=0, tiled=True)  7.37 us
    ppermute x3, starting transfers between devices, along_line(): return lax.ppermute(bundles[step], 'pool', pairs)  5.02 us
    pallas_call x1, Pallas kernels, shards(): pl.pallas_call(functools.partial(plan_kernel, cap, chunk, devices), out_s...  4.74 us
    all_to_all x1, waiting for transfers between devices, shards(): lax.all_to_all(sending, 'pool', split_axis=0, concat_axis=0, tiled=True)  4.15 us
    pallas_call x1, Pallas kernels, shards(): pl.pallas_call(functools.partial(decode_kernel, layout, chunk, width), ou...  3.95 us
    all_to_all x1, starting transfers between devices, shards(): lax.all_to_all(answers, 'pool', split_axis=0, concat_axis=0, tiled=True)  3.59 us
    all_to_all x1, waiting for transfers between devices, shards(): lax.all_to_all(answers, 'pool', split_axis=0, concat_axis=0, tiled=True)  3.36 us
  transfers between devices with their start and end apart: 8, of which 5 were waited for; matrix products, arithmetic and copies ran while one was open for 0% of the time, Pallas kernels for 40%

profile of v6, /device:TPU:0, one launch (start us, length us, event | category | flops | bytes accessed | tf_op | source)
XLA Modules:
  0.0 55.8 jit_solution(1867476890218336512)
XLA Ops:
  0.6 2.3 %pack.1 = bf16[4,4,160,128]{3,2,1,0:T(8,128)(2,1)} custom-call(s32[256]{0:T(256)} %bitcast.9, bf16[16,8192]{1,0:T(8,128)(2,1)} %q.1, bf16[16,2048]{1,0:T(8,128)(2,1)} %kv.1), custom_call_target="tpu_custom_call" | custom-call | tf_op jit(solution)/shard_map/pack/pallas_call | solution.py:414
  2.9 7.4 %all-to-all-start = ((bf16[16,160,128]{2,1,0:T(8,128)(2,1)}), bf16[16,160,128]{2,1,0:T(8,128)(2,1)S(1)}, u32[]{:S(2)}, u32[]{:S(2)}) async-start(bf16[16,160,128]{2,1,0:T(8,128)(2,1)} %bitcast.8), calls=%async_computation | async-start | bytes 1310720 | tf_op jit(solution)/shard_map/all_to_all | solution.py:430
  10.3 2.3 %blocks.1 = (bf16[2,2,2,16,256]{4,3,2,1,0:T(8,128)(2,1)S(1)}, bf16[2,2,2,16,256]{4,3,2,1,0:T(8,128)(2,1)S(1)}, bf16[2,2,2,16,256]{4,3,2,1,0:T(8,128)(2,1)S(1)}, bf16[2,2,2,16,256]{4,3,2,1,0:T(8,128)(2,1)S(1)}) custom-call(s32[2,32]{1,0:T(2,128)} %table.3, s32[2]{0:T(128)} %count.3, bf16[4,8,16,256]{3,2,1,0:T(8,128)(2,1)} %pool.1), custom_call_target="tpu_custom_call" | custom-call | flops 100000 | bytes 1000000 | tf_op jit(solution)/shard_map/blocks/pallas_call | solution.py:435
  12.6 0.5 collective-permute-start
  13.0 1.7 %collective-permute-start.1 = (bf16[2,2,2,16,256]{4,3,2,1,0:T(8,128)(2,1)S(1)}, bf16[2,2,2,16,256]{4,3,2,1,0:T(8,128)(2,1)S(1)}, u32[]{:S(2)}, u32[]{:S(2)}) collective-permute-start(bf16[2,2,2,16,256]{4,3,2,1,0:T(8,128)(2,1)S(1)} %get-tuple-element.34), channel_id=1, source_target_pairs={{0,2},{1,3},{2,0},{3,1},{4,6},{5,7},{6,4},{7,5},{8,10},{9,11},{10,... | collective-permute-start | bytes 196616 | tf_op jit(solution)/shard_map/ppermute | solution.py:446
  14.7 0.0 collective-permute-start.2
  14.7 4.7 %plan.1 = (s32[128]{0:T(128)S(1)}, s32[34]{0:T(128)S(1)}, s32[64]{0:T(128)S(1)}, bf16[32,2,64,256]{3,2,1,0:T(8,128)(2,1)S(1)}) custom-call(s32[2,32]{1,0:T(2,128)} %table.3, s32[2]{0:T(128)} %count.3, s32[256]{0:T(256)} %bitcast.10, s32[256]{0:T(256)} %lengths.1, bf16[128,2,64,256]{3,2,1,0:T(8,128)(2,1)} %bitcast.6), custom_call_target="tpu_custom_call" | custom-call | flops 1000000 | bytes 4000000 | tf_op jit(solution)/shard_map/plan/pallas_call | solution.py:452
  19.5 0.0 collective-permute-done.rest_1_
  19.5 0.0 collective-permute-done.1.rest_2_
  19.5 1.7 %collective-permute-done.2.rest_3_ = bf16[2,2,2,16,256]{4,3,2,1,0:T(8,128)(2,1)S(1)} collective-permute-done((bf16[2,2,2,16,256]{4,3,2,1,0:T(8,128)(2,1)S(1)}, bf16[2,2,2,16,256]{4,3,2,1,0:T(8,128)(2,1)S(1)}, u32[]{:S(2)}, u32[]{:S(2)}) %collective-permute-start.2) | collective-permute-done | bytes 65568 | tf_op jit(solution)/shard_map/ppermute | solution.py:446
  21.2 0.5 regroup.1
  21.7 1.3 %collective-permute-start.3 = (bf16[4,2,16,256]{3,2,1,0:T(8,128)(2,1)S(1)}, bf16[4,2,16,256]{3,2,1,0:T(8,128)(2,1)S(1)}, u32[]{:S(2)}, u32[]{:S(2)}) collective-permute-start(bf16[4,2,16,256]{3,2,1,0:T(8,128)(2,1)S(1)} %get-tuple-element.45), channel_id=1, source_target_pairs={{0,4},{1,5},{2,6},{3,7},{4,0},{5,1},{6,2},{7,3},{8,12},{9,13},{10,... | collective-permute-start | bytes 196616 | tf_op jit(solution)/shard_map/ppermute | solution.py:486
  23.0 4.2 %all-to-all-done.recv = bf16[16,160,128]{2,1,0:T(8,128)(2,1)S(1)} async-done(((bf16[16,160,128]{2,1,0:T(8,128)(2,1)}), bf16[16,160,128]{2,1,0:T(8,128)(2,1)S(1)}, u32[]{:S(2)}, u32[]{:S(2)}) %all-to-all-start) | async-done | bytes 655392 | tf_op jit(solution)/shard_map/all_to_all | solution.py:430
  27.2 2.6 %collective-permute-start.4 = (bf16[4,2,16,256]{3,2,1,0:T(8,128)(2,1)S(1)}, bf16[4,2,16,256]{3,2,1,0:T(8,128)(2,1)S(1)}, u32[]{:S(2)}, u32[]{:S(2)}) collective-permute-start(bf16[4,2,16,256]{3,2,1,0:T(8,128)(2,1)S(1)} %get-tuple-element.52), channel_id=1, source_target_pairs={{0,8},{1,9},{2,10},{3,11},{4,12},{5,13},{6,14},{7,15},{8,0},{9,1},... | collective-permute-start | bytes 196616 | tf_op jit(solution)/shard_map/ppermute | solution.py:486
  29.8 1.1 %collective-permute-start.5 = (bf16[4,2,16,256]{3,2,1,0:T(8,128)(2,1)S(1)}, bf16[4,2,16,256]{3,2,1,0:T(8,128)(2,1)S(1)}, u32[]{:S(2)}, u32[]{:S(2)}) collective-permute-start(bf16[4,2,16,256]{3,2,1,0:T(8,128)(2,1)S(1)} %get-tuple-element.53), channel_id=1, source_target_pairs={{0,12},{1,13},{2,14},{3,15},{4,8},{5,9},{6,10},{7,11},{8,4},{9,5},... | collective-permute-start | bytes 196616 | tf_op jit(solution)/shard_map/ppermute | solution.py:486
  30.9 3.9 %decode.1 = bf16[16,128,128]{2,1,0:T(8,128)(2,1)} custom-call(s32[34]{0:T(128)S(1)} %get-tuple-element.48.listed, s32[128]{0:T(128)S(1)} %get-tuple-element.49.slot_len, bf16[16,160,128]{2,1,0:T(8,128)(2,1)S(1)} %all-to-all-done.recv, bf16[32,2,64,256]{3,2,1,0:T(8,128)(2,1)S(1)} %get-tuple-element.51.ahead, bf16[128,2,64,256]{3,2,1,0:T(8,128)(2,1)} %bitcast.7), custom_call_target="tpu_custom_call" | custom-call | flops 500000000 | bytes 8000000 | tf_op jit(solution)/shard_map/decode/pallas_call | solution.py:495
  34.8 0.0 collective-permute-done.3.rest_1_
  34.8 0.3 collective-permute-done.4.rest_2_
  35.1 0.8 %collective-permute-done.5.rest_3_ = bf16[4,2,16,256]{3,2,1,0:T(8,128)(2,1)S(1)} collective-permute-done((bf16[4,2,16,256]{3,2,1,0:T(8,128)(2,1)S(1)}, bf16[4,2,16,256]{3,2,1,0:T(8,128)(2,1)S(1)}, u32[]{:S(2)}, u32[]{:S(2)}) %collective-permute-start.5) | collective-permute-done | bytes 65568 | tf_op jit(solution)/shard_map/ppermute | solution.py:486
  36.0 3.6 %all-to-all-start.1 = ((bf16[16,128,128]{2,1,0:T(8,128)(2,1)}), bf16[16,128,128]{2,1,0:T(8,128)(2,1)S(1)}, u32[]{:S(2)}, u32[]{:S(2)}) async-start(bf16[16,128,128]{2,1,0:T(8,128)(2,1)} %decode.1), calls=%async_computation.1 | async-start | bytes 1048576 | tf_op jit(solution)/shard_map/all_to_all | solution.py:512
  39.6 11.1 %prefill.1 = bf16[512,1024]{1,0:T(8,128)(2,1)} custom-call(s32[64]{0:T(128)S(1)} %get-tuple-element.55.prefix_held, bf16[4,2,16,256]{3,2,1,0:T(8,128)(2,1)S(1)} %get-tuple-element.56.rest_0_, bf16[4,2,16,256]{3,2,1,0:T(8,128)(2,1)S(1)} %collective-permute-done.3.rest_1_, bf16[4,2,16,256]{3,2,1,0:T(8,128)(2,1)S(1)} %collective-permute-done.4.rest_2_, ...), custom_call_target="tpu_custom_call" | custom-call | flops 1610612736 | bytes 3000000 | tf_op jit(solution)/shard_map/prefill/pallas_call | solution.py:518
  50.7 3.4 %all-to-all-done.1.back = bf16[16,128,128]{2,1,0:T(8,128)(2,1)S(1)} async-done(((bf16[16,128,128]{2,1,0:T(8,128)(2,1)}), bf16[16,128,128]{2,1,0:T(8,128)(2,1)S(1)}, u32[]{:S(2)}, u32[]{:S(2)}) %all-to-all-start.1) | async-done | bytes 524320 | tf_op jit(solution)/shard_map/all_to_all | solution.py:512
  54.0 1.8 %unpack.1 = bf16[16,8192]{1,0:T(8,128)(2,1)} custom-call(s32[256]{0:T(256)} %bitcast.11, bf16[16,128,128]{2,1,0:T(8,128)(2,1)S(1)} %all-to-all-done.1.back), custom_call_target="tpu_custom_call" | custom-call | tf_op jit(solution)/shard_map/unpack/pallas_call | solution.py:543
Async XLA Ops:
  2.9 24.3 %all-to-all-start = ((bf16[16,160,128]{2,1,0:T(8,128)(2,1)}), bf16[16,160,128]{2,1,0:T(8,128)(2,1)S(1)}, u32[]{:S(2)}, u32[]{:S(2)}) async-start(bf16[16,160,128]{2,1,0:T(8,128)(2,1)} %bitcast.8), calls=%async_computation | async-start | bytes 1310720 | tf_op jit(solution)/shard_map/all_to_all | solution.py:430
  12.6 6.9 %collective-permute-start = (bf16[2,2,2,16,256]{4,3,2,1,0:T(8,128)(2,1)S(1)}, bf16[2,2,2,16,256]{4,3,2,1,0:T(8,128)(2,1)S(1)}, u32[]{:S(2)}, u32[]{:S(2)}) collective-permute-start(bf16[2,2,2,16,256]{4,3,2,1,0:T(8,128)(2,1)S(1)} %get-tuple-element.33), channel_id=1, source_target_pairs={{0,1},{1,0},{2,3},{3,2},{4,5},{5,4},{6,7},{7,6},{8,9},{9,8},{10,11... | collective-permute-start | bytes 196616 | tf_op jit(solution)/shard_map/ppermute | solution.py:446
  13.0 6.4 %collective-permute-start.1 = (bf16[2,2,2,16,256]{4,3,2,1,0:T(8,128)(2,1)S(1)}, bf16[2,2,2,16,256]{4,3,2,1,0:T(8,128)(2,1)S(1)}, u32[]{:S(2)}, u32[]{:S(2)}) collective-permute-start(bf16[2,2,2,16,256]{4,3,2,1,0:T(8,128)(2,1)S(1)} %get-tuple-element.34), channel_id=1, source_target_pairs={{0,2},{1,3},{2,0},{3,1},{4,6},{5,7},{6,4},{7,5},{8,10},{9,11},{10,... | collective-permute-start | bytes 196616 | tf_op jit(solution)/shard_map/ppermute | solution.py:446
  14.7 6.4 %collective-permute-start.2 = (bf16[2,2,2,16,256]{4,3,2,1,0:T(8,128)(2,1)S(1)}, bf16[2,2,2,16,256]{4,3,2,1,0:T(8,128)(2,1)S(1)}, u32[]{:S(2)}, u32[]{:S(2)}) collective-permute-start(bf16[2,2,2,16,256]{4,3,2,1,0:T(8,128)(2,1)S(1)} %get-tuple-element.35), channel_id=1, source_target_pairs={{0,3},{1,2},{2,1},{3,0},{4,7},{5,6},{6,5},{7,4},{8,11},{9,10},{10,... | collective-permute-start | bytes 196616 | tf_op jit(solution)/shard_map/ppermute | solution.py:446
  21.7 13.1 %collective-permute-start.3 = (bf16[4,2,16,256]{3,2,1,0:T(8,128)(2,1)S(1)}, bf16[4,2,16,256]{3,2,1,0:T(8,128)(2,1)S(1)}, u32[]{:S(2)}, u32[]{:S(2)}) collective-permute-start(bf16[4,2,16,256]{3,2,1,0:T(8,128)(2,1)S(1)} %get-tuple-element.45), channel_id=1, source_target_pairs={{0,4},{1,5},{2,6},{3,7},{4,0},{5,1},{6,2},{7,3},{8,12},{9,13},{10,... | collective-permute-start | bytes 196616 | tf_op jit(solution)/shard_map/ppermute | solution.py:486
  27.2 8.0 %collective-permute-start.4 = (bf16[4,2,16,256]{3,2,1,0:T(8,128)(2,1)S(1)}, bf16[4,2,16,256]{3,2,1,0:T(8,128)(2,1)S(1)}, u32[]{:S(2)}, u32[]{:S(2)}) collective-permute-start(bf16[4,2,16,256]{3,2,1,0:T(8,128)(2,1)S(1)} %get-tuple-element.52), channel_id=1, source_target_pairs={{0,8},{1,9},{2,10},{3,11},{4,12},{5,13},{6,14},{7,15},{8,0},{9,1},... | collective-permute-start | bytes 196616 | tf_op jit(solution)/shard_map/ppermute | solution.py:486
  29.8 6.2 %collective-permute-start.5 = (bf16[4,2,16,256]{3,2,1,0:T(8,128)(2,1)S(1)}, bf16[4,2,16,256]{3,2,1,0:T(8,128)(2,1)S(1)}, u32[]{:S(2)}, u32[]{:S(2)}) collective-permute-start(bf16[4,2,16,256]{3,2,1,0:T(8,128)(2,1)S(1)} %get-tuple-element.53), channel_id=1, source_target_pairs={{0,12},{1,13},{2,14},{3,15},{4,8},{5,9},{6,10},{7,11},{8,4},{9,5},... | collective-permute-start | bytes 196616 | tf_op jit(solution)/shard_map/ppermute | solution.py:486
  36.0 18.1 %all-to-all-start.1 = ((bf16[16,128,128]{2,1,0:T(8,128)(2,1)}), bf16[16,128,128]{2,1,0:T(8,128)(2,1)S(1)}, u32[]{:S(2)}, u32[]{:S(2)}) async-start(bf16[16,128,128]{2,1,0:T(8,128)(2,1)} %decode.1), calls=%async_computation.1 | async-start | bytes 1048576 | tf_op jit(solution)/shard_map/all_to_all | solution.py:512
